TPU v7x, 256 devices: a whole 4x4x8 slice. The times are simulated.
256 devices in a mesh: tile: 64 (over z_lo, x, y), pos: 4 (over z_hi, core).
Axes of the slice: x: 4, y: 4, z: 8 (z_hi: 2, z_lo: 4; z = z_hi * 4 + z_lo), core: 2. Of those that a mesh axis runs over, the one named last changes fastest.
Arguments:
- object_tiles: float32 [64, 2, 512, 512], P('tile'), may hold values from -5 to 5
- probe: float32 [2, 256, 256], replicated, may hold values from -6 to 6
- patterns: bfloat16 [2048, 256, 256], P(('tile', 'pos')), may hold values from 0 to 4
- corners: int32 [2048, 2], P(('tile', 'pos')), may hold values from 0 to 511, as said below
- counts: int32 [256], P(('tile', 'pos')), may hold values from 1 to 7, as said below
Outputs:
- refined: float32 [64, 2, 512, 512], P('tile')
Inputs may be any that keep to these rules, and one draw needn't show every extreme that they name: `corners`: tile t sits in grid cell (t + 8 + 8 // 2) mod 64 of a row-major grid of 8 tiles a row. A corner row is at most 256 for slots of tiles in the grid's last row, a corner column at most 256 for slots of tiles in the grid's last column, so every crop lies inside the object. The device at tile index t and the one at tile index t + 32 with the same pos index have counts that sum to exactly 8; some device has 7.
All inputs are finite; a program needn't handle non-finite values.
Results may differ from a plain program's by a relative error of at most 0.018.
Values may be sent and summed in bfloat16 or wider, within the bound.
A program may use at most 64 MiB of HBM per device.

v0:
```python
import math

import jax
import jax.numpy as jnp
from jax import lax
from jax.sharding import PartitionSpec as P

TILE_COLS = 8
ITERS = 2


LEARNING_RATE = 0.03


def from_behind(value, axis, steps):
    count = lax.axis_size(axis)
    pairs = [(source, (source + steps) % count) for source in range(count)]
    return lax.ppermute(value, axis, pairs)


def for_sending(x):

    def short(part):
        return part.astype(jnp.bfloat16) if part.dtype == jnp.float32 else part

    return jax.tree.map(short, x)


def tables(extent):
    counter = jnp.arange(extent, dtype=jnp.int32)
    phases = counter[:, None] * counter[None, :] % extent
    angles = phases.astype(jnp.float32) * (2.0 * math.pi / extent)
    factor = 1.0 / math.sqrt(extent)
    cosine = jnp.cos(angles) * factor
    sine_neg = -jnp.sin(angles) * factor
    forward_right = jnp.concatenate(
        [jnp.concatenate([cosine, sine_neg], 1), jnp.concatenate([-sine_neg, cosine], 1)], 0
    ).astype(jnp.bfloat16)
    forward_left = jnp.concatenate([cosine, sine_neg], 0).astype(jnp.bfloat16)
    backward_right = jnp.concatenate(
        [jnp.concatenate([cosine, -sine_neg], 1), jnp.concatenate([sine_neg, cosine], 1)], 0
    ).astype(jnp.bfloat16)
    backward_left = jnp.concatenate([cosine, -sine_neg], 0).astype(jnp.bfloat16)
    return (forward_right, forward_left, backward_right, backward_left)


def transform(waves, right_table, left_table):
    number, extent = (waves.shape[0], waves.shape[1])
    halfway = jnp.dot(
        waves.reshape(number * extent, 2 * extent), right_table, preferred_element_type=jnp.float32
    )
    halfway = halfway.reshape(number, extent, 2 * extent).astype(jnp.bfloat16)
    stacked = jnp.einsum("jk,skl->sjl", left_table, halfway, preferred_element_type=jnp.float32)
    upper = stacked[:, :extent]
    lower = stacked[:, extent:]
    real_part = upper[:, :, :extent] - lower[:, :, extent:]
    imag_part = upper[:, :, extent:] + lower[:, :, :extent]
    return jnp.concatenate([real_part, imag_part], 2)


def wave_gradient(waves, measured, table_set):
    extent = waves.shape[1]
    spectrum = transform(waves, table_set[0], table_set[1])
    power = spectrum[:, :, :extent] ** 2 + spectrum[:, :, extent:] ** 2
    misfit = power - measured.astype(jnp.float32)
    pushed = (spectrum * jnp.concatenate([misfit, misfit], 2)).astype(jnp.bfloat16)
    return transform(pushed, table_set[2], table_set[3]).astype(jnp.bfloat16)


def exit_waves(probe, crops):
    real_part = probe[0] * crops[:, 0] - probe[1] * crops[:, 1]
    imag_part = probe[0] * crops[:, 1] + probe[1] * crops[:, 0]
    return jnp.concatenate([real_part, imag_part], 2).astype(jnp.bfloat16)


def crop_gradients(probe, wave_grads, alive_mask):
    extent = probe.shape[1]
    real_in = wave_grads[:, :, :extent].astype(jnp.float32)
    imag_in = wave_grads[:, :, extent:].astype(jnp.float32)
    real_part = probe[0] * real_in + probe[1] * imag_in
    imag_part = probe[0] * imag_in - probe[1] * real_in
    return jnp.stack([real_part, imag_part], 1) * alive_mask[:, None, None, None]


def extend_tile(object_tile, keep_right, keep_down, extent):
    right_piece = (
        from_behind(object_tile[:, :, :extent].astype(jnp.bfloat16), "tile", -1).astype(jnp.float32)
        * keep_right
    )
    lower_piece = (
        from_behind(object_tile[:, :extent, :].astype(jnp.bfloat16), "tile", -TILE_COLS).astype(
            jnp.float32
        )
        * keep_down
    )
    corner_piece = from_behind(for_sending(lower_piece[:, :, :extent]), "tile", -1) * keep_right
    upper_band = jnp.concatenate([object_tile, right_piece], 2)
    lower_band = jnp.concatenate([lower_piece, corner_piece], 2)
    return jnp.concatenate([upper_band, lower_band], 1)


def fold_margins(extended_grad, keep_left, keep_up, extent, tile_edge):
    interior = extended_grad[:, :tile_edge, :tile_edge]
    right_in = (
        from_behind(
            extended_grad[:, :tile_edge, tile_edge:].astype(jnp.bfloat16), "tile", 1
        ).astype(jnp.float32)
        * keep_left
    )
    bottom_band = extended_grad[:, tile_edge:, :tile_edge]
    corner_in = (
        from_behind(
            extended_grad[:, tile_edge:, tile_edge:].astype(jnp.bfloat16), "tile", 1
        ).astype(jnp.float32)
        * keep_left
    )
    bottom_band = bottom_band.at[:, :, :extent].add(corner_in)
    lower_in = (
        from_behind(bottom_band.astype(jnp.bfloat16), "tile", TILE_COLS).astype(bottom_band.dtype)
        * keep_up
    )
    interior = interior.at[:, :, :extent].add(right_in)
    interior = interior.at[:, :extent, :].add(lower_in)
    return interior


def shards(object_tiles, probe, patterns, corners, counts):
    object_tile = object_tiles[0]
    extent = probe.shape[1]
    tile_edge = object_tile.shape[1]
    slot_total = patterns.shape[0]
    table_set = tables(extent)
    tile_count = lax.axis_size("tile")
    grid_rows = tile_count // TILE_COLS
    cell_at = (lax.axis_index("tile") + TILE_COLS + TILE_COLS // 2) % tile_count
    column_at = cell_at % TILE_COLS
    row_at_grid = cell_at // TILE_COLS
    keep_right = (column_at != TILE_COLS - 1).astype(jnp.float32)
    keep_left = (column_at != 0).astype(jnp.float32)
    keep_down = (row_at_grid != grid_rows - 1).astype(jnp.float32)
    keep_up = (row_at_grid != 0).astype(jnp.float32)
    live_count = counts[0]
    slot_order = jnp.arange(slot_total, dtype=jnp.int32)
    alive_mask = (slot_order < live_count).astype(jnp.float32)
    corner_rows = corners[:, 0]
    corner_cols = corners[:, 1]
    zero_index = jnp.zeros((), jnp.int32)
    for repeat in range(ITERS):
        extended = extend_tile(object_tile, keep_right, keep_down, extent)

        def cut_window(row_at, col_at):
            return lax.dynamic_slice(extended, (zero_index, row_at, col_at), (2, extent, extent))

        crops = jax.vmap(cut_window)(corner_rows, corner_cols)
        waves = exit_waves(probe, crops)
        wave_grads = wave_gradient(waves, patterns, table_set)
        slot_grads = crop_gradients(probe, wave_grads, alive_mask)

        def add_slot(position, running):
            anchor = (zero_index, corner_rows[position], corner_cols[position])
            region = lax.dynamic_slice(running, anchor, (2, extent, extent))
            return lax.dynamic_update_slice(running, region + slot_grads[position], anchor)

        extended_grad = lax.fori_loop(
            0, slot_total, add_slot, jnp.zeros(extended.shape, jnp.float32)
        )
        tile_grad = fold_margins(extended_grad, keep_left, keep_up, extent, tile_edge)
        object_tile = object_tile - LEARNING_RATE * lax.psum(
            tile_grad.astype(jnp.bfloat16), "pos"
        ).astype(jnp.float32)
    return object_tile[None]


def solution(mesh):
    return jax.shard_map(
        shards,
        mesh=mesh,
        in_specs=(
            P("tile", None, None, None),
            P(),
            P(("tile", "pos"), None, None),
            P(("tile", "pos"), None),
            P(("tile", "pos")),
        ),
        out_specs=P("tile", None, None, None),
        check_vma=False,
    )
```

profile of v0, /device:TPU:1, one launch (start us, length us, event | category | flops | bytes accessed | tf_op | source)
XLA Modules:
  0.0 704.3 jit_solution(13892477144413400388)
XLA Ops:
  9.2 7.6 %collective-permute-start.1 = (bf16[2,256,512]{2,1,0:T(8,128)(2,1)}, bf16[2,256,512]{2,1,0:T(8,128)(2,1)}, u32[]{:S(2)}, u32[]{:S(2)}) collective-permute-start(bf16[2,256,512]{2,1,0:T(8,128)(2,1)} %slice.405), channel_id=1, source_target_pairs={{0,224},{4,228},{8,232},{12,236},{16,240},{20,244},{24,248},{28,25... | collective-permute-start | bytes 1572872 | tf_op jit(solution)/shard_map/ppermute | solution.py:18
  29.1 8.7 %collective-permute-start.2 = (bf16[2,256,256]{2,1,0:T(8,128)(2,1)S(1)}, bf16[2,256,256]{2,1,0:T(8,128)(2,1)S(1)}, u32[]{:S(2)}, u32[]{:S(2)}) collective-permute-start(bf16[2,256,256]{2,1,0:T(8,128)(2,1)S(1)} %slice.487), channel_id=1, source_target_pairs={{0,252},{4,0},{8,4},{12,8},{16,12},{20,16},{24,20},{28,24},{32,28}... | collective-permute-start | bytes 786440 | tf_op jit(solution)/shard_map/ppermute | solution.py:18
  49.5 35.5 %while.36 = (s32[]{:T(128)}, f32[2,768,768]{2,1,0:T(8,128)}, s32[8,3]{0,1:T(4,128)S(1)}, f32[8,2,256,256]{2,3,0,1:T(8,128)}, s32[]{:T(128)}) while((s32[]{:T(128)}, f32[2,768,768]{2,1,0:T(8,128)}, s32[8,3]{0,1:T(4,128)S(1)}, f32[8,2,256,256]{2,3,0,1:T(8,128)}, s32[]{:T(128)}) %tuple.121), condition=%wide.while_cond.6, body=%wide.while_body.6.sunk | while | flops 2 | bytes 3146353 | solution.py:152
  89.2 7.4 %convolution_bitcast_fusion.3 = f32[8,512,512]{1,2,0:T(8,128)} fusion(bf16[8,256,256]{1,2,0:T(8,128)(2,1)} %get-tuple-element.350, bf16[8,256,256]{1,2,0:T(8,128)(2,1)} %get-tuple-element.349, bf16[256,256]{1,0:T(8,128)(2,1)S(1)} %get-tuple-element.358, bf16[256,256]{1,0:T(8,128)(2,1)} %get-tuple-element.357, bf16[256,256]{1,0:T(8,128)(2,1)} %fusion.80), kind=kOutput, calls=%fused_computation.21 | convolution fusion | flops 2155347968 | bytes 10878976 | tf_op jit(solution)/shard_map/jk,skl->sjl/dot_general | solution.py:53
  96.5 6.6 convert_subtract_fusion.1
  103.1 9.2 %convolution_bitcast_fusion.2 = f32[8,512,512]{1,2,0:T(8,128)} fusion(f32[8,256,256]{1,2,0:T(8,128)} %get-tuple-element.342, f32[8,256,256]{1,2,0:T(8,128)} %get-tuple-element.341, f32[8,256,256]{1,2,0:T(8,128)} %get-tuple-element.340, bf16[256,256]{1,0:T(8,128)(2,1)S(1)} %get-tuple-element.358, bf16[256,256]{1,0:T(8,128)(2,1)} %fusion.80, ...), kind=kOutput, calls=%fused_computation.20 | convolution fusion | flops 2155347968 | bytes 15073280 | tf_op jit(solution)/shard_map/jk,skl->sjl/dot_general | solution.py:53
  122.1 114.6 %while.34 = (s32[]{:T(128)}, f32[2,768,768]{2,1,0:T(8,128)}, s32[8]{0:T(128)S(1)}, s32[8]{0:T(128)S(1)}, f32[8,2,256,256]{2,3,0,1:T(8,128)}, /*index=5*/s32[]{:T(128)}, s32[]{:T(128)}, s32[]{:T(128)}) while((s32[]{:T(128)}, f32[2,768,768]{2,1,0:T(8,128)}, s32[8]{0:T(128)S(1)}, s32[8]{0:T(128)S(1)}, f32[8,2,256,256]{2,3,0,1:T(8,128)}, ...), condition=%wide.region_1.2_spmd, body=%wide.region_0.1_spmd.sunk | while | flops 131080 | bytes 4718785 | solution.py:164
  129.9 6.5 dynamic_update_slice.16
  144.2 6.8 dynamic_update_slice.16
  158.6 6.8 dynamic_update_slice.16
  173.1 6.6 dynamic_update_slice.16
  187.5 6.5 dynamic_update_slice.16
  201.7 6.8 dynamic_update_slice.16
  216.2 6.8 dynamic_update_slice.16
  241.5 11.6 %collective-permute-done.4 = bf16[2,256,256]{2,1,0:T(8,128)(2,1)} collective-permute-done((bf16[2,256,256]{2,1,0:T(8,128)(2,1)}, bf16[2,256,256]{2,1,0:T(8,128)(2,1)}, u32[]{:S(2)}, u32[]{:S(2)}) %collective-permute-start.4) | collective-permute-done | bytes 262176 | tf_op jit(solution)/shard_map/ppermute | solution.py:18
  256.4 13.7 %collective-permute-done.3 = bf16[2,512,256]{2,1,0:T(8,128)(2,1)} collective-permute-done((bf16[2,512,256]{2,1,0:T(8,128)(2,1)S(1)}, bf16[2,512,256]{2,1,0:T(8,128)(2,1)}, u32[]{:S(2)}, u32[]{:S(2)}) %collective-permute-start.3) | collective-permute-done | bytes 524320 | tf_op jit(solution)/shard_map/ppermute | solution.py:18
  274.2 78.7 %all-reduce.3.cloned.1.call-done = bf16[2,512,512]{2,1,0:T(8,128)(2,1)} async-done(((bf16[2,512,512]{2,1,0:T(8,128)(2,1)}), bf16[2,512,512]{2,1,0:T(8,128)(2,1)}) %all-reduce.3.cloned.1.call-update) | async-done | bytes 1048592 | tf_op jit(solution)/shard_map/psum | solution.py:168
  361.4 10.3 %collective-permute-done.7 = bf16[2,256,512]{2,1,0:T(8,128)(2,1)} collective-permute-done((bf16[2,256,512]{2,1,0:T(8,128)(2,1)}, bf16[2,256,512]{2,1,0:T(8,128)(2,1)}, u32[]{:S(2)}, u32[]{:S(2)}) %collective-permute-start.7) | collective-permute-done | bytes 524320 | tf_op jit(solution)/shard_map/ppermute | solution.py:18
  391.5 35.5 %while.37 = (s32[]{:T(128)}, f32[2,768,768]{2,1,0:T(8,128)}, s32[8,3]{0,1:T(4,128)S(1)}, f32[8,2,256,256]{2,3,0,1:T(8,128)}, s32[]{:T(128)}) while((s32[]{:T(128)}, f32[2,768,768]{2,1,0:T(8,128)}, s32[8,3]{0,1:T(4,128)S(1)}, f32[8,2,256,256]{2,3,0,1:T(8,128)}, s32[]{:T(128)}) %tuple.137), condition=%wide.while_cond.7, body=%wide.while_body.7.sunk | while | flops 2 | bytes 3146353 | solution.py:152
  431.1 7.4 %convolution_bitcast_fusion.1 = f32[8,512,512]{1,2,0:T(8,128)} fusion(bf16[8,256,256]{1,2,0:T(8,128)(2,1)} %get-tuple-element.348, bf16[8,256,256]{1,2,0:T(8,128)(2,1)} %get-tuple-element.347, bf16[256,256]{1,0:T(8,128)(2,1)S(1)} %get-tuple-element.358, bf16[256,256]{1,0:T(8,128)(2,1)} %get-tuple-element.357, bf16[256,256]{1,0:T(8,128)(2,1)} %fusion.80), kind=kOutput, calls=%fused_computation.19 | convolution fusion | flops 2155347968 | bytes 10878976 | tf_op jit(solution)/shard_map/jk,skl->sjl/dot_general | solution.py:53
  438.5 6.6 convert_subtract_fusion
  445.1 9.2 %convolution_bitcast_fusion = f32[8,512,512]{1,2,0:T(8,128)} fusion(f32[8,256,256]{1,2,0:T(8,128)} %get-tuple-element.334, f32[8,256,256]{1,2,0:T(8,128)} %get-tuple-element.333, f32[8,256,256]{1,2,0:T(8,128)} %get-tuple-element.332, bf16[256,256]{1,0:T(8,128)(2,1)S(1)} %get-tuple-element.358, bf16[256,256]{1,0:T(8,128)(2,1)} %fusion.80, ...), kind=kOutput, calls=%fused_computation.18 | convolution fusion | flops 2155347968 | bytes 15073280 | tf_op jit(solution)/shard_map/jk,skl->sjl/dot_general | solution.py:53
  464.1 114.6 %while.35 = (s32[]{:T(128)}, f32[2,768,768]{2,1,0:T(8,128)}, s32[8]{0:T(128)S(1)}, s32[8]{0:T(128)S(1)}, f32[8,2,256,256]{2,3,0,1:T(8,128)}, /*index=5*/s32[]{:T(128)}, s32[]{:T(128)}, s32[]{:T(128)}) while((s32[]{:T(128)}, f32[2,768,768]{2,1,0:T(8,128)}, s32[8]{0:T(128)S(1)}, s32[8]{0:T(128)S(1)}, f32[8,2,256,256]{2,3,0,1:T(8,128)}, ...), condition=%wide.region_4.5_spmd, body=%wide.region_3.4_spmd.sunk | while | flops 131080 | bytes 4718785 | solution.py:164
  471.8 6.5 dynamic_update_slice.17
  486.1 6.8 dynamic_update_slice.17
  500.6 6.8 dynamic_update_slice.17
  515.1 6.6 dynamic_update_slice.17
  543.7 6.8 dynamic_update_slice.17
  558.2 6.8 dynamic_update_slice.17
  582.6 12.3 %collective-permute-done.10 = bf16[2,256,256]{2,1,0:T(8,128)(2,1)S(1)} collective-permute-done((bf16[2,256,256]{2,1,0:T(8,128)(2,1)S(1)}, bf16[2,256,256]{2,1,0:T(8,128)(2,1)S(1)}, u32[]{:S(2)}, u32[]{:S(2)}) %collective-permute-start.10) | collective-permute-done | bytes 262176 | tf_op jit(solution)/shard_map/ppermute | solution.py:18
  596.3 13.3 %collective-permute-done.9 = bf16[2,512,256]{2,1,0:T(8,128)(2,1)S(1)} collective-permute-done((bf16[2,512,256]{2,1,0:T(8,128)(2,1)S(1)}, bf16[2,512,256]{2,1,0:T(8,128)(2,1)S(1)}, u32[]{:S(2)}, u32[]{:S(2)}) %collective-permute-start.9) | collective-permute-done | bytes 524320 | tf_op jit(solution)/shard_map/ppermute | solution.py:18
  611.3 83.2 %all-reduce.5.cloned.1.call-done = bf16[2,512,512]{2,1,0:T(8,128)(2,1)} async-done(((bf16[2,512,512]{2,1,0:T(8,128)(2,1)}), bf16[2,512,512]{2,1,0:T(8,128)(2,1)}) %all-reduce.5.cloned.1.call-update) | async-done | bytes 1048592 | tf_op jit(solution)/shard_map/psum | solution.py:168
  (261 shorter events, 254.3 us)
Async XLA Ops:
  6.5 14.4 %copy-start.8 = (f32[2,256,256]{2,1,0:T(8,128)S(1)}, f32[2,256,256]{2,1,0:T(8,128)}, u32[]{:S(2)}) copy-start(f32[2,256,256]{2,1,0:T(8,128)} %param.22) | copy-start | bytes 1572868
  6.5 346.4 %all-reduce.3.cloned.1.call-start = ((), (), s32[]{:S(2)}) async-start(), calls=%async_computation | async-start | bytes 2097152 | tf_op jit(solution)/shard_map/psum | solution.py:168
  8.3 12.7 %copy-start.9 = (s32[8,2]{0,1:T(2,128)S(1)}, s32[8,2]{0,1:T(2,128)}, u32[]{:S(2)}) copy-start(s32[8,2]{0,1:T(2,128)} %param.24) | copy-start | bytes 196
  8.3 14.4 %copy-start.7 = (bf16[8,256,256]{2,1,0:T(8,128)(2,1)S(1)}, bf16[8,256,256]{2,1,0:T(8,128)(2,1)}, u32[]{:S(2)}) copy-start(bf16[8,256,256]{2,1,0:T(8,128)(2,1)} %param.23) | copy-start | bytes 3145732
  9.2 18.5 %collective-permute-start.1 = (bf16[2,256,512]{2,1,0:T(8,128)(2,1)}, bf16[2,256,512]{2,1,0:T(8,128)(2,1)}, u32[]{:S(2)}, u32[]{:S(2)}) collective-permute-start(bf16[2,256,512]{2,1,0:T(8,128)(2,1)} %slice.405), channel_id=1, source_target_pairs={{0,224},{4,228},{8,232},{12,236},{16,240},{20,244},{24,248},{28,25... | collective-permute-start | bytes 1572872 | tf_op jit(solution)/shard_map/ppermute | solution.py:18
  17.6 21.3 %collective-permute-start = (bf16[2,512,256]{2,1,0:T(8,128)(2,1)}, bf16[2,512,256]{2,1,0:T(8,128)(2,1)}, u32[]{:S(2)}, u32[]{:S(2)}) collective-permute-start(bf16[2,512,256]{2,1,0:T(8,128)(2,1)} %slice.404), channel_id=1, source_target_pairs={{0,252},{4,0},{8,4},{12,8},{16,12},{20,16},{24,20},{28,24},{32,28}... | collective-permute-start | bytes 1572872 | tf_op jit(solution)/shard_map/ppermute | solution.py:18
  27.4 17.1 %copy-start.1 = (f32[1,2,512,512]{3,2,1,0:T(8,128)S(1)}, f32[1,2,512,512]{3,2,1,0:T(8,128)}, u32[]{:S(2)}) copy-start(f32[1,2,512,512]{3,2,1,0:T(8,128)} %param.21) | copy-start | bytes 6291460
  29.1 15.4 %collective-permute-start.2 = (bf16[2,256,256]{2,1,0:T(8,128)(2,1)S(1)}, bf16[2,256,256]{2,1,0:T(8,128)(2,1)S(1)}, u32[]{:S(2)}, u32[]{:S(2)}) collective-permute-start(bf16[2,256,256]{2,1,0:T(8,128)(2,1)S(1)} %slice.487), channel_id=1, source_target_pairs={{0,252},{4,0},{8,4},{12,8},{16,12},{20,16},{24,20},{28,24},{32,28}... | collective-permute-start | bytes 786440 | tf_op jit(solution)/shard_map/ppermute | solution.py:18
  89.2 7.4 %copy-start.5 = (bf16[8,256,256]{1,2,0:T(8,128)(2,1)S(1)}, bf16[8,256,256]{1,2,0:T(8,128)(2,1)}, u32[]{:S(2)}) copy-start(bf16[8,256,256]{1,2,0:T(8,128)(2,1)} %copy.10) | copy-start | bytes 3145732
  103.1 9.2 %copy-start.3 = (f32[256,256]{0,1:T(8,128)S(1)}, f32[256,256]{0,1:T(8,128)}, u32[]{:S(2)}) copy-start(f32[256,256]{0,1:T(8,128)} %copy.8) | copy-start | bytes 786436
  240.1 13.0 %collective-permute-start.4 = (bf16[2,256,256]{2,1,0:T(8,128)(2,1)}, bf16[2,256,256]{2,1,0:T(8,128)(2,1)}, u32[]{:S(2)}, u32[]{:S(2)}) collective-permute-start(bf16[2,256,256]{2,1,0:T(8,128)(2,1)} %slice.417), channel_id=1, source_target_pairs={{0,4},{4,8},{8,12},{12,16},{16,20},{20,24},{24,28},{28,32},{32,36}... | collective-permute-start | bytes 786440 | tf_op jit(solution)/shard_map/ppermute | solution.py:18
  240.1 30.0 %collective-permute-start.3 = (bf16[2,512,256]{2,1,0:T(8,128)(2,1)S(1)}, bf16[2,512,256]{2,1,0:T(8,128)(2,1)}, u32[]{:S(2)}, u32[]{:S(2)}) collective-permute-start(bf16[2,512,256]{2,1,0:T(8,128)(2,1)S(1)} %slice.415), channel_id=1, source_target_pairs={{0,4},{4,8},{8,12},{12,16},{16,20},{20,24},{24,28},{28,32},{32,36}... | collective-permute-start | bytes 1572872 | tf_op jit(solution)/shard_map/ppermute | solution.py:18
  254.3 17.4 %collective-permute-start.5 = (bf16[2,256,512]{2,1,0:T(8,128)(2,1)S(1)}, bf16[2,256,512]{2,1,0:T(8,128)(2,1)}, u32[]{:S(2)}, u32[]{:S(2)}) collective-permute-start(bf16[2,256,512]{2,1,0:T(8,128)(2,1)S(1)} %add_dynamic-update-slice_fusion.3), channel_id=1, source_target_pairs={{0,32},{4,36},{8,40},{12,44},{16,48},{20,52},{24,56},{28,60},{32,6... | collective-permute-start | bytes 1572872 | tf_op jit(solution)/shard_map/ppermute | solution.py:18
  274.2 420.3 %all-reduce.5.cloned.1.call-start = ((), (), s32[]{:S(2)}) async-start(), calls=%async_computation.1 | async-start | bytes 2097152 | tf_op jit(solution)/shard_map/psum | solution.py:168
  356.8 14.9 %collective-permute-start.7 = (bf16[2,256,512]{2,1,0:T(8,128)(2,1)}, bf16[2,256,512]{2,1,0:T(8,128)(2,1)}, u32[]{:S(2)}, u32[]{:S(2)}) collective-permute-start(bf16[2,256,512]{2,1,0:T(8,128)(2,1)} %slice.419), channel_id=1, source_target_pairs={{0,224},{4,228},{8,232},{12,236},{16,240},{20,244},{24,248},{28,25... | collective-permute-start | bytes 1572872 | tf_op jit(solution)/shard_map/ppermute | solution.py:18
  358.2 22.6 %collective-permute-start.6 = (bf16[2,512,256]{2,1,0:T(8,128)(2,1)S(1)}, bf16[2,512,256]{2,1,0:T(8,128)(2,1)S(1)}, u32[]{:S(2)}, u32[]{:S(2)}) collective-permute-start(bf16[2,512,256]{2,1,0:T(8,128)(2,1)S(1)} %slice.418), channel_id=1, source_target_pairs={{0,252},{4,0},{8,4},{12,8},{16,12},{20,16},{24,20},{28,24},{32,28}... | collective-permute-start | bytes 1572872 | tf_op jit(solution)/shard_map/ppermute | solution.py:18
  361.4 25.1 %copy-start.2 = (f32[2,512,512]{2,1,0:T(8,128)S(1)}, f32[2,512,512]{2,1,0:T(8,128)}, u32[]{:S(2)}) copy-start(f32[2,512,512]{2,1,0:T(8,128)} %get-tuple-element.336) | copy-start | bytes 6291460
  372.9 13.6 %collective-permute-start.8 = (bf16[2,256,256]{2,1,0:T(8,128)(2,1)S(1)}, bf16[2,256,256]{2,1,0:T(8,128)(2,1)S(1)}, u32[]{:S(2)}, u32[]{:S(2)}) collective-permute-start(bf16[2,256,256]{2,1,0:T(8,128)(2,1)S(1)} %slice.486), channel_id=1, source_target_pairs={{0,252},{4,0},{8,4},{12,8},{16,12},{20,16},{24,20},{28,24},{32,28}... | collective-permute-start | bytes 786440 | tf_op jit(solution)/shard_map/ppermute | solution.py:18
  431.1 7.4 %copy-start.6 = (bf16[8,256,256]{1,2,0:T(8,128)(2,1)S(1)}, bf16[8,256,256]{1,2,0:T(8,128)(2,1)}, u32[]{:S(2)}) copy-start(bf16[8,256,256]{1,2,0:T(8,128)(2,1)} %copy.10) | copy-start | bytes 3145732
  445.1 9.2 %copy-start.4 = (f32[256,256]{0,1:T(8,128)S(1)}, f32[256,256]{0,1:T(8,128)}, u32[]{:S(2)}) copy-start(f32[256,256]{0,1:T(8,128)} %copy.8) | copy-start | bytes 786436
  578.8 3.8 copy-start
  581.5 13.4 %collective-permute-start.10 = (bf16[2,256,256]{2,1,0:T(8,128)(2,1)S(1)}, bf16[2,256,256]{2,1,0:T(8,128)(2,1)S(1)}, u32[]{:S(2)}, u32[]{:S(2)}) collective-permute-start(bf16[2,256,256]{2,1,0:T(8,128)(2,1)S(1)} %slice.431), channel_id=1, source_target_pairs={{0,4},{4,8},{8,12},{12,16},{16,20},{20,24},{24,28},{28,32},{32,36}... | collective-permute-start | bytes 786440 | tf_op jit(solution)/shard_map/ppermute | solution.py:18
  581.6 28.1 %collective-permute-start.9 = (bf16[2,512,256]{2,1,0:T(8,128)(2,1)S(1)}, bf16[2,512,256]{2,1,0:T(8,128)(2,1)S(1)}, u32[]{:S(2)}, u32[]{:S(2)}) collective-permute-start(bf16[2,512,256]{2,1,0:T(8,128)(2,1)S(1)} %slice.429), channel_id=1, source_target_pairs={{0,4},{4,8},{8,12},{12,16},{16,20},{20,24},{24,28},{28,32},{32,36}... | collective-permute-start | bytes 1572872 | tf_op jit(solution)/shard_map/ppermute | solution.py:18
  595.0 14.9 %collective-permute-start.11 = (bf16[2,256,512]{2,1,0:T(8,128)(2,1)S(1)}, bf16[2,256,512]{2,1,0:T(8,128)(2,1)S(1)}, u32[]{:S(2)}, u32[]{:S(2)}) collective-permute-start(bf16[2,256,512]{2,1,0:T(8,128)(2,1)S(1)} %add_dynamic-update-slice_fusion.2), channel_id=1, source_target_pairs={{0,32},{4,36},{8,40},{12,44},{16,48},{20,52},{24,56},{28,60},{32,6... | collective-permute-start | bytes 1572872 | tf_op jit(solution)/shard_map/ppermute | solution.py:18
Sparse Core Ops, SparseCore 0:
  274.3 78.5 all-reduce.2
  611.4 83.0 all-reduce.4
where the time goes:
time: 711 us; the launch traced here: 704 us
  waiting for transfers between devices  236 us (33%)
  local copies, waits for them, and re-layouts  235 us (33%)
  other arithmetic  90.1 us (13%)
  loops' own time  62.6 us (9%)
  matrix products  33.2 us (5%)
  starting transfers between devices  32.3 us (5%)
  between operations  14.4 us (2%)
    psum x2, waiting for transfers between devices, shards(): lax.psum(tile_grad.astype(jnp.bfloat16), 'pos').astype(jnp.float32)  162 us
    dynamic_update_slice x16, local copies, waits for them, and re-layouts, add_slot(): lax.dynamic_update_slice(running, region + slot_grads[position], anchor)  106 us
    ppermute x12, waiting for transfers between devices, from_behind(): return lax.ppermute(value, axis, pairs)  74.2 us
    gather x80, local copies, waits for them, and re-layouts  70.9 us
    another operation x2, loops' own time, shards(): lax.fori_loop(0, slot_total, add_slot, jnp.zeros(extended.shape, jnp.floa...  62.5 us
    dot_general x4, matrix products, transform(): jnp.einsum('jk,skl->sjl', left_table, halfway, preferred_element_type=jnp...  33.2 us
    ppermute x12, starting transfers between devices, from_behind(): return lax.ppermute(value, axis, pairs)  32.3 us
    add x16, other arithmetic, add_slot(): region + slot_grads[position]  21.9 us
  transfers between devices with their start and end apart: 14, of which 12 were waited for; matrix products, arithmetic and copies ran while one was open for 2% of the time, Pallas kernels for 0%

commit v1 on v0

v1 whole, which is shorter than its diff:
```python
import functools
import math

import jax
import jax.numpy as jnp
import numpy as np
from jax import lax
from jax.experimental import pallas as pl
from jax.experimental.pallas import tpu as pltpu
from jax.sharding import PartitionSpec as P

TILE_COLS = 8
ITERS = 2
LEARNING_RATE = 0.03
LANES = 128
SUBLANES = 8
CHUNK = 32


def tables(extent):
    counter = np.arange(extent, dtype=np.int64)
    phases = counter[:, None] * counter[None, :] % extent
    angles = phases.astype(np.float64) * (2.0 * math.pi / extent)
    factor = 1.0 / math.sqrt(extent)
    cosine = np.cos(angles) * factor
    sine_neg = -np.sin(angles) * factor
    first = np.block([[cosine, sine_neg], [-sine_neg, cosine]])
    second = np.block([[cosine, -sine_neg], [sine_neg, cosine]])
    return jnp.asarray(first, jnp.bfloat16), jnp.asarray(second, jnp.bfloat16)


def slots_kernel(
    corners, counts, tile, right, lower, diag, probe, patterns, first, second,
    grad_tile, grad_right, grad_lower, grad_diag,
    image, grad, padded, rolled, wave, half, spectrum,
):
    extent = probe.shape[1]
    edge = tile.shape[1]
    own = edge // LANES
    margin = extent // LANES
    f32 = jnp.float32
    for ch in range(2):
        for b in range(own):
            cols = slice(b * LANES, (b + 1) * LANES)
            image[b, ch, :edge] = tile[ch, :, cols]
            image[b, ch, edge:] = lower[ch, :, cols].astype(f32)
        for b in range(margin):
            cols = slice(b * LANES, (b + 1) * LANES)
            image[own + b, ch, :edge] = right[ch, :, cols].astype(f32)
            image[own + b, ch, edge:] = diag[ch, :, cols].astype(f32)
        for b in range(margin):
            cols = slice(b * LANES, (b + 1) * LANES)
            padded[ch, b, :SUBLANES] = probe[ch, extent - SUBLANES:, cols]
            padded[ch, b, SUBLANES:] = probe[ch, :, cols]
    grad[...] = jnp.zeros_like(grad)

    def slot(g, carry):
        row = corners[g, 0]
        col = corners[g, 1]
        row_off = lax.rem(row, SUBLANES)
        col_off = lax.rem(col, LANES)
        row_at = pl.multiple_of(row - row_off, SUBLANES)
        block = lax.div(col, LANES)
        lane = lax.broadcasted_iota(jnp.int32, (CHUNK, LANES), 1)
        keep = lane >= col_off
        lane8 = lax.broadcasted_iota(jnp.int32, (SUBLANES, LANES), 1)
        sub8 = lax.broadcasted_iota(jnp.int32, (SUBLANES, LANES), 0)
        keep8 = lane8 >= col_off
        stay8 = sub8 >= row_off
        over = pl.multiple_of(row_at + extent, SUBLANES)

        for i in range(0, extent, CHUNK):
            here = slice(i, i + CHUNK)
            shifted = []
            for ch in range(2):
                turned = [
                    pltpu.roll(
                        padded[ch, b, pl.ds(SUBLANES - row_off + i, CHUNK), :], col_off, 1
                    )
                    for b in range(2)
                ]
                shifted.append(
                    (jnp.where(keep, turned[0], turned[1]), jnp.where(keep, turned[1], turned[0]))
                )
                rolled[ch, 0, here] = shifted[ch][0]
                rolled[ch, 1, here] = shifted[ch][1]
            rows = pl.ds(pl.multiple_of(row_at + i, SUBLANES), CHUNK)
            crops = []
            for ch in range(2):
                left = jnp.where(keep, image[block, ch, rows, :], image[block + 2, ch, rows, :])
                mid = image[block + 1, ch, rows, :]
                if i == 0:
                    below = pl.ds(over, SUBLANES)
                    left8 = jnp.where(
                        keep8, image[block, ch, below, :], image[block + 2, ch, below, :]
                    )
                    mid8 = image[block + 1, ch, below, :]
                    left = jnp.concatenate(
                        [jnp.where(stay8, left[:SUBLANES], left8), left[SUBLANES:]], 0
                    )
                    mid = jnp.concatenate(
                        [jnp.where(stay8, mid[:SUBLANES], mid8), mid[SUBLANES:]], 0
                    )
                crops.append((left, mid))
            for b in range(2):
                real = shifted[0][b] * crops[0][b] - shifted[1][b] * crops[1][b]
                imag = shifted[0][b] * crops[1][b] + shifted[1][b] * crops[0][b]
                wave[here, b * LANES:(b + 1) * LANES] = real.astype(jnp.bfloat16)
                wave[here, extent + b * LANES:extent + (b + 1) * LANES] = imag.astype(jnp.bfloat16)

        def rightwards(table):
            result = jnp.dot(wave[...], table[...], preferred_element_type=f32)
            half[:extent] = result[:, :extent].astype(jnp.bfloat16)
            half[extent:] = result[:, extent:].astype(jnp.bfloat16)

        def downwards(table):
            spectrum[...] = jnp.dot(table[...], half[...], preferred_element_type=f32)

        rightwards(first)
        downwards(second)
        for i in range(0, extent, CHUNK):
            here = slice(i, i + CHUNK)
            real = spectrum[here]
            imag = spectrum[extent + i:extent + i + CHUNK]
            misfit = real * real + imag * imag - patterns[g, here].astype(f32)
            wave[here, :extent] = (real * misfit).astype(jnp.bfloat16)
            wave[here, extent:] = (imag * misfit).astype(jnp.bfloat16)
        rightwards(second)
        downwards(first)

        for i in range(0, extent, CHUNK):
            here = slice(i, i + CHUNK)
            rows = pl.ds(pl.multiple_of(row_at + i, SUBLANES), CHUNK)
            for b in range(2):
                cols = slice(b * LANES, (b + 1) * LANES)
                real = spectrum[here, cols]
                imag = spectrum[extent + i:extent + i + CHUNK, cols]
                p_real = rolled[0, b, here]
                p_imag = rolled[1, b, here]
                parts = (p_real * real + p_imag * imag, p_real * imag - p_imag * real)
                for ch in range(2):
                    value = parts[ch]
                    if i == 0:
                        spill = jnp.where(stay8, 0.0, value[:SUBLANES])
                        value = jnp.concatenate(
                            [jnp.where(stay8, value[:SUBLANES], 0.0), value[SUBLANES:]], 0
                        )
                        below = pl.ds(over, SUBLANES)
                        if b == 0:
                            grad[block, ch, below, :] += jnp.where(keep8, spill, 0.0)
                            grad[block + 2, ch, below, :] += jnp.where(keep8, 0.0, spill)
                        else:
                            grad[block + 1, ch, below, :] += spill
                    if b == 0:
                        grad[block, ch, rows, :] += jnp.where(keep, value, 0.0)
                        grad[block + 2, ch, rows, :] += jnp.where(keep, 0.0, value)
                    else:
                        grad[block + 1, ch, rows, :] += value
        return carry

    lax.fori_loop(0, counts[0], slot, 0)

    for ch in range(2):
        for b in range(own):
            cols = slice(b * LANES, (b + 1) * LANES)
            grad_tile[ch, :, cols] = grad[b, ch, :edge].astype(jnp.bfloat16)
            grad_lower[ch, :, cols] = grad[b, ch, edge:].astype(jnp.bfloat16)
        for b in range(margin):
            cols = slice(b * LANES, (b + 1) * LANES)
            grad_right[ch, :, cols] = grad[own + b, ch, :edge].astype(jnp.bfloat16)
            grad_diag[ch, :, cols] = grad[own + b, ch, edge:].astype(jnp.bfloat16)


def slot_gradients(tile, right, lower, diag, probe, patterns, corners, counts, first, second):
    extent = probe.shape[1]
    edge = tile.shape[1]
    total = edge + extent
    blocks = total // LANES
    f32, bf16 = jnp.float32, jnp.bfloat16
    vmem = pl.BlockSpec(memory_space=pltpu.VMEM)
    smem = pl.BlockSpec(memory_space=pltpu.SMEM)
    return pl.pallas_call(
        slots_kernel,
        out_shape=(
            jax.ShapeDtypeStruct((2, edge, edge), bf16),
            jax.ShapeDtypeStruct((2, edge, extent), bf16),
            jax.ShapeDtypeStruct((2, extent, edge), bf16),
            jax.ShapeDtypeStruct((2, extent, extent), bf16),
        ),
        in_specs=[smem, smem] + [vmem] * 8,
        out_specs=(vmem,) * 4,
        scratch_shapes=[
            pltpu.VMEM((blocks, 2, total, LANES), f32),
            pltpu.VMEM((blocks, 2, total, LANES), f32),
            pltpu.VMEM((2, 2, extent + SUBLANES, LANES), f32),
            pltpu.VMEM((2, 2, extent, LANES), f32),
            pltpu.VMEM((extent, 2 * extent), bf16),
            pltpu.VMEM((2 * extent, extent), bf16),
            pltpu.VMEM((2 * extent, extent), f32),
        ],
        compiler_params=pltpu.CompilerParams(vmem_limit_bytes=40 * 1024 * 1024),
        cost_estimate=pl.CostEstimate(
            flops=4 * 4 * 2 * extent**3 * 2, bytes_accessed=8 * 2**20, transcendentals=0
        ),
    )(corners, counts, tile, right, lower, diag, probe, patterns, first, second)


def shifted_by(value, steps):
    count = lax.axis_size("tile")
    return lax.ppermute(value, "tile", [(s, (s + steps) % count) for s in range(count)])


def shards(object_tiles, probe, patterns, corners, counts):
    tile = object_tiles[0]
    extent = probe.shape[1]
    first, second = tables(extent)
    for repeat in range(ITERS):
        short = tile.astype(jnp.bfloat16)
        right = shifted_by(short[:, :, :extent], -1)
        lower = shifted_by(short[:, :extent, :], -TILE_COLS)
        diag = shifted_by(short[:, :extent, :extent], -TILE_COLS - 1)
        grads = slot_gradients(
            tile, right, lower, diag, probe, patterns, corners, counts, first, second
        )
        total, *margins = grads
        total = total.astype(jnp.float32)
        right_in = shifted_by(margins[0], 1).astype(jnp.float32)
        lower_in = shifted_by(margins[1], TILE_COLS).astype(jnp.float32)
        diag_in = shifted_by(margins[2], TILE_COLS + 1).astype(jnp.float32)
        total = total.at[:, :, :extent].add(right_in)
        total = total.at[:, :extent, :].add(lower_in)
        total = total.at[:, :extent, :extent].add(diag_in)
        tile = tile - LEARNING_RATE * lax.psum(total.astype(jnp.bfloat16), "pos").astype(
            jnp.float32
        )
    return tile[None]


def solution(mesh):
    return jax.shard_map(
        shards,
        mesh=mesh,
        in_specs=(
            P("tile", None, None, None),
            P(),
            P(("tile", "pos"), None, None),
            P(("tile", "pos"), None),
            P(("tile", "pos")),
        ),
        out_specs=P("tile", None, None, None),
        check_vma=False,
    )
```

time: 711 us -> 348 us (0.49)
  local copies, waits for them, and re-layouts: 235 us -> 5.74 us
  other arithmetic: 90.1 us -> 10.6 us
  loops' own time: 62.6 us -> 0 us
  waiting for transfers between devices: 236 us -> 279 us
  matrix products: 33.2 us -> 0 us
  Pallas kernels: 0 us -> 20.3 us
  starting transfers between devices: 32.3 us -> 17.8 us
    dynamic_update_slice x16 -> x0, local copies, waits for them, and re-layouts: 106 us -> none  [add_slot(): lax.dynamic_update_slice(running, region + slot_grads[position], anchor)]
    gather x80 -> x0, local copies, waits for them, and re-layouts: 70.9 us -> none
    another operation x4 -> x0, loops' own time: 62.6 us -> none  [the longest x2 62.5 us: shards(): lax.fori_loop(0, slot_total, add_slot, jnp.zeros(extended.shape, jnp.floa...]
    ppermute x12, waiting for transfers between devices: 74.2 us -> 118 us  [shifted_by(): lax.ppermute(value, 'tile', [(s, (s + steps) % count) for s in range(coun...]
    dynamic_slice x64 -> x0, local copies, waits for them, and re-layouts: 39.3 us -> none  [the longest x32 20.5 us: add_slot(): slot_grads[position]]
    dot_general x4 -> x0, matrix products: 33.2 us -> none  [transform(): jnp.einsum('jk,skl->sjl', left_table, halfway, preferred_element_type=jnp...]
    another operation x12 -> x0, other arithmetic: 31.2 us -> none
    add x16 -> x0, other arithmetic: 21.9 us -> none  [add_slot(): region + slot_grads[position]]
  transfers between devices with their start and end apart: 14 -> 14, of which waited for: 12 -> 6; matrix products, arithmetic and copies ran while one was open for 2% -> 1% of each run, Pallas kernels for 0% -> 0%
where the time goes in v1:
time: 348 us
  waiting for transfers between devices  279 us (80%)
  Pallas kernels  20.3 us (6%)
  starting transfers between devices  17.8 us (5%)
  between operations  14.4 us (4%)
  other arithmetic  10.6 us (3%)
  local copies, waits for them, and re-layouts  5.74 us (2%)
    psum x2, waiting for transfers between devices, shards(): lax.psum(total.astype(jnp.bfloat16), 'pos').astype(jnp.float32)  161 us
    ppermute x12, waiting for transfers between devices, shifted_by(): lax.ppermute(value, 'tile', [(s, (s + steps) % count) for s in range(coun...  118 us
    pallas_call x2, Pallas kernels, slot_gradients(): pl.pallas_call(slots_kernel, out_shape=(jax.ShapeDtypeStruct((2, edge, ed...  20.3 us
    ppermute x12, starting transfers between devices, shifted_by(): lax.ppermute(value, 'tile', [(s, (s + steps) % count) for s in range(coun...  17.8 us
  transfers between devices with their start and end apart: 14, of which 6 were waited for; matrix products, arithmetic and copies ran while one was open for 1% of the time, Pallas kernels for 0%

profile of v1, /device:TPU:1, one launch (start us, length us, event | category | flops | bytes accessed | tf_op | source)
XLA Modules:
  0.0 348.0 jit_solution(14124186907730783504)
XLA Ops:
  6.5 1.8 bitcast_convert_fusion
  8.4 0.8 slice.184
  9.2 9.8 %collective-permute-start = (bf16[2,512,256]{2,1,0:T(8,128)(2,1)}, bf16[2,512,256]{2,1,0:T(8,128)(2,1)}, u32[]{:S(2)}, u32[]{:S(2)}) collective-permute-start(bf16[2,512,256]{2,1,0:T(8,128)(2,1)} %slice.184), channel_id=1, source_target_pairs={{0,252},{4,0},{8,4},{12,8},{16,12},{20,16},{24,20},{28,24},{32,28}... | collective-permute-start | bytes 1572872 | tf_op jit(solution)/shard_map/ppermute | solution.py:210
  19.0 0.8 slice.185
  19.9 0.5 collective-permute-start.1
  20.4 0.8 slice.186
  21.9 37.0 %collective-permute-done.2.diag = bf16[2,256,256]{2,1,0:T(8,128)(2,1)S(1)} collective-permute-done((bf16[2,256,256]{2,1,0:T(8,128)(2,1)}, bf16[2,256,256]{2,1,0:T(8,128)(2,1)S(1)}, u32[]{:S(2)}, u32[]{:S(2)}) %collective-permute-start.2) | collective-permute-done | bytes 262176 | tf_op jit(solution)/shard_map/ppermute | solution.py:210
  59.0 1.0 copy-done.4
  60.0 1.0 copy-done.6
  61.1 1.0 copy-done.8
  62.1 10.4 %shard_map.73 = (bf16[2,512,512]{2,1,0:T(8,128)(2,1)S(1)}, bf16[2,512,256]{2,1,0:T(8,128)(2,1)S(1)}, bf16[2,256,512]{2,1,0:T(8,128)(2,1)S(1)}, bf16[2,256,256]{2,1,0:T(8,128)(2,1)S(1)}) custom-call(s32[8,2]{1,0:T(8,128)S(1)} %copy.8.corners, s32[1]{0:T(128)S(6)} %copy.18.counts, f32[2,512,512]{2,1,0:T(8,128)S(1)} %bitcast.6, ...), custom_call_target="tpu_custom_call" | custom-call | flops 1073741824 | bytes 8388608 | tf_op jit(solution)/shard_map/pallas_call | solution.py:182
  72.8 0.3 convert_element_type.43
  73.1 21.3 %collective-permute-done.3 = bf16[2,512,256]{2,1,0:T(8,128)(2,1)S(1)} collective-permute-done((bf16[2,512,256]{2,1,0:T(8,128)(2,1)S(1)}, bf16[2,512,256]{2,1,0:T(8,128)(2,1)S(1)}, u32[]{:S(2)}, u32[]{:S(2)}) %collective-permute-start.3) | collective-permute-done | bytes 524320 | tf_op jit(solution)/shard_map/ppermute | solution.py:210
  94.4 0.2 fusion.1
  94.6 0.4 constant_dynamic-update-slice_fusion.1
  95.0 0.1 fusion.3
  95.1 1.1 convert_element_type.47
  96.3 81.2 %all-reduce.3.cloned.1.call-done = bf16[2,512,512]{2,1,0:T(8,128)(2,1)} async-done(((bf16[2,512,512]{2,1,0:T(8,128)(2,1)}), bf16[2,512,512]{2,1,0:T(8,128)(2,1)}) %all-reduce.3.cloned.1.call-update) | async-done | bytes 1048592 | tf_op jit(solution)/shard_map/psum | solution.py:233
  177.5 1.7 fusion.4
  179.3 3.4 collective-permute-start.6
  182.7 0.6 collective-permute-start.7
  183.3 2.9 collective-permute-start.8
  186.2 37.5 %collective-permute-done.8.diag = bf16[2,256,256]{2,1,0:T(8,128)(2,1)S(1)} collective-permute-done((bf16[2,256,256]{2,1,0:T(8,128)(2,1)S(1)}, bf16[2,256,256]{2,1,0:T(8,128)(2,1)S(1)}, u32[]{:S(2)}, u32[]{:S(2)}) %collective-permute-start.8) | collective-permute-done | bytes 262176 | tf_op jit(solution)/shard_map/ppermute | solution.py:210
  223.8 9.9 %shard_map.74 = (bf16[2,512,512]{2,1,0:T(8,128)(2,1)S(1)}, bf16[2,512,256]{2,1,0:T(8,128)(2,1)S(1)}, bf16[2,256,512]{2,1,0:T(8,128)(2,1)S(1)}, bf16[2,256,256]{2,1,0:T(8,128)(2,1)S(1)}) custom-call(s32[8,2]{1,0:T(8,128)S(1)} %copy.8.corners, s32[1]{0:T(128)S(6)} %copy.18.counts, f32[2,512,512]{2,1,0:T(8,128)S(1)} %get-tuple-element.96.tile, ...), custom_call_target="tpu_custom_call" | custom-call | flops 1073741824 | bytes 8388608 | tf_op jit(solution)/shard_map/pallas_call | solution.py:182
  234.0 0.3 convert_element_type.50
  234.3 21.9 %collective-permute-done.9 = bf16[2,512,256]{2,1,0:T(8,128)(2,1)S(1)} collective-permute-done((bf16[2,512,256]{2,1,0:T(8,128)(2,1)S(1)}, bf16[2,512,256]{2,1,0:T(8,128)(2,1)S(1)}, u32[]{:S(2)}, u32[]{:S(2)}) %collective-permute-start.9) | collective-permute-done | bytes 524320 | tf_op jit(solution)/shard_map/ppermute | solution.py:210
  256.2 0.2 fusion
  256.4 0.3 constant_dynamic-update-slice_fusion
  256.8 0.1 fusion.2
  256.9 1.1 convert_element_type.54
  258.0 80.2 %all-reduce.5.cloned.1.call-done = bf16[2,512,512]{2,1,0:T(8,128)(2,1)} async-done(((bf16[2,512,512]{2,1,0:T(8,128)(2,1)}), bf16[2,512,512]{2,1,0:T(8,128)(2,1)}) %all-reduce.5.cloned.1.call-update) | async-done | bytes 1048592 | tf_op jit(solution)/shard_map/psum | solution.py:233
  338.2 2.9 subtract_bitcast_fusion
  (42 shorter events, 0.9 us)
Async XLA Ops:
  6.5 170.9 %all-reduce.3.cloned.1.call-start = ((), (), s32[]{:S(2)}) async-start(), calls=%async_computation | async-start | bytes 2097152 | tf_op jit(solution)/shard_map/psum | solution.py:233
  6.5 52.4 %copy-start.3 = (bf16[8,256,256]{2,1,0:T(8,128)(2,1)S(1)}, bf16[8,256,256]{2,1,0:T(8,128)(2,1)}, u32[]{:S(2)}) copy-start(bf16[8,256,256]{2,1,0:T(8,128)(2,1)} %patterns.3) | copy-start | bytes 3145732
  8.4 13.5 %copy-start.10 = (s32[8,2]{0,1:T(2,128)S(1)}, s32[8,2]{0,1:T(2,128)}, u32[]{:S(2)}) copy-start(s32[8,2]{0,1:T(2,128)} %param.22) | copy-start | bytes 196
  8.4 50.6 %copy-start = (f32[1,2,512,512]{3,2,1,0:T(8,128)S(1)}, f32[1,2,512,512]{3,2,1,0:T(8,128)}, u32[]{:S(2)}) copy-start(f32[1,2,512,512]{3,2,1,0:T(8,128)} %param.19) | copy-start | bytes 6291460
  9.2 49.8 %collective-permute-start = (bf16[2,512,256]{2,1,0:T(8,128)(2,1)}, bf16[2,512,256]{2,1,0:T(8,128)(2,1)}, u32[]{:S(2)}, u32[]{:S(2)}) collective-permute-start(bf16[2,512,256]{2,1,0:T(8,128)(2,1)} %slice.184), channel_id=1, source_target_pairs={{0,252},{4,0},{8,4},{12,8},{16,12},{20,16},{24,20},{28,24},{32,28}... | collective-permute-start | bytes 1572872 | tf_op jit(solution)/shard_map/ppermute | solution.py:210
  19.9 39.1 %collective-permute-start.1 = (bf16[2,256,512]{2,1,0:T(8,128)(2,1)}, bf16[2,256,512]{2,1,0:T(8,128)(2,1)}, u32[]{:S(2)}, u32[]{:S(2)}) collective-permute-start(bf16[2,256,512]{2,1,0:T(8,128)(2,1)} %slice.185), channel_id=1, source_target_pairs={{0,224},{4,228},{8,232},{12,236},{16,240},{20,244},{24,248},{28,25... | collective-permute-start | bytes 1572872 | tf_op jit(solution)/shard_map/ppermute | solution.py:210
  21.1 37.8 %collective-permute-start.2 = (bf16[2,256,256]{2,1,0:T(8,128)(2,1)}, bf16[2,256,256]{2,1,0:T(8,128)(2,1)S(1)}, u32[]{:S(2)}, u32[]{:S(2)}) collective-permute-start(bf16[2,256,256]{2,1,0:T(8,128)(2,1)} %slice.186), channel_id=1, source_target_pairs={{0,220},{4,224},{8,228},{12,232},{16,236},{20,240},{24,244},{28,24... | collective-permute-start | bytes 786440 | tf_op jit(solution)/shard_map/ppermute | solution.py:210
  59.0 1.0 copy-start.4
  60.0 1.0 copy-start.6
  61.1 1.0 copy-start.8
  72.5 21.9 %collective-permute-start.3 = (bf16[2,512,256]{2,1,0:T(8,128)(2,1)S(1)}, bf16[2,512,256]{2,1,0:T(8,128)(2,1)S(1)}, u32[]{:S(2)}, u32[]{:S(2)}) collective-permute-start(bf16[2,512,256]{2,1,0:T(8,128)(2,1)S(1)} %get-tuple-element.86), channel_id=1, source_target_pairs={{0,4},{4,8},{8,12},{12,16},{16,20},{20,24},{24,28},{28,32},{32,36}... | collective-permute-start | bytes 1572872 | tf_op jit(solution)/shard_map/ppermute | solution.py:210
  72.6 22.0 %collective-permute-start.4 = (bf16[2,256,512]{2,1,0:T(8,128)(2,1)S(1)}, bf16[2,256,512]{2,1,0:T(8,128)(2,1)S(1)}, u32[]{:S(2)}, u32[]{:S(2)}) collective-permute-start(bf16[2,256,512]{2,1,0:T(8,128)(2,1)S(1)} %get-tuple-element.87), channel_id=1, source_target_pairs={{0,32},{4,36},{8,40},{12,44},{16,48},{20,52},{24,56},{28,60},{32,6... | collective-permute-start | bytes 1572872 | tf_op jit(solution)/shard_map/ppermute | solution.py:210
  72.7 22.3 %collective-permute-start.5 = (bf16[2,256,256]{2,1,0:T(8,128)(2,1)S(1)}, bf16[2,256,256]{2,1,0:T(8,128)(2,1)S(1)}, u32[]{:S(2)}, u32[]{:S(2)}) collective-permute-start(bf16[2,256,256]{2,1,0:T(8,128)(2,1)S(1)} %get-tuple-element.88), channel_id=1, source_target_pairs={{0,36},{4,40},{8,44},{12,48},{16,52},{20,56},{24,60},{28,64},{32,6... | collective-permute-start | bytes 786440 | tf_op jit(solution)/shard_map/ppermute | solution.py:210
  96.3 242.0 %all-reduce.5.cloned.1.call-start = ((), (), s32[]{:S(2)}) async-start(), calls=%async_computation.1 | async-start | bytes 2097152 | tf_op jit(solution)/shard_map/psum | solution.py:233
  179.2 54.6 %copy-start.1 = (f32[2,512,512]{2,1,0:T(8,128)}, f32[2,512,512]{2,1,0:T(8,128)S(1)}, u32[]{:S(2)}) copy-start(f32[2,512,512]{2,1,0:T(8,128)S(1)} %get-tuple-element.96.tile) | copy-start | bytes 6291460
  179.2 44.6 %copy-start.5 = (f32[2,256,256]{2,1,0:T(8,128)S(1)}, f32[2,256,256]{2,1,0:T(8,128)}, u32[]{:S(2)}) copy-start(f32[2,256,256]{2,1,0:T(8,128)} %probe.3) | copy-start | bytes 1572868
  179.2 44.6 %copy-start.7 = (bf16[512,512]{1,0:T(8,128)(2,1)S(1)}, bf16[512,512]{1,0:T(8,128)(2,1)}, u32[]{:S(2)}) copy-start(bf16[512,512]{1,0:T(8,128)(2,1)} %constant.149.clone.second) | copy-start | bytes 1572868
  179.2 44.6 %copy-start.9 = (bf16[512,512]{1,0:T(8,128)(2,1)S(1)}, bf16[512,512]{1,0:T(8,128)(2,1)}, u32[]{:S(2)}) copy-start(bf16[512,512]{1,0:T(8,128)(2,1)} %constant.148.clone.first) | copy-start | bytes 1572868
  179.3 44.5 %collective-permute-start.6 = (bf16[2,512,256]{2,1,0:T(8,128)(2,1)S(1)}, bf16[2,512,256]{2,1,0:T(8,128)(2,1)S(1)}, u32[]{:S(2)}, u32[]{:S(2)}) collective-permute-start(bf16[2,512,256]{2,1,0:T(8,128)(2,1)S(1)} %slice.190), channel_id=1, source_target_pairs={{0,252},{4,0},{8,4},{12,8},{16,12},{20,16},{24,20},{28,24},{32,28}... | collective-permute-start | bytes 1572872 | tf_op jit(solution)/shard_map/ppermute | solution.py:210
  182.7 41.0 %collective-permute-start.7 = (bf16[2,256,512]{2,1,0:T(8,128)(2,1)S(1)}, bf16[2,256,512]{2,1,0:T(8,128)(2,1)S(1)}, u32[]{:S(2)}, u32[]{:S(2)}) collective-permute-start(bf16[2,256,512]{2,1,0:T(8,128)(2,1)S(1)} %slice.191), channel_id=1, source_target_pairs={{0,224},{4,228},{8,232},{12,236},{16,240},{20,244},{24,248},{28,25... | collective-permute-start | bytes 1572872 | tf_op jit(solution)/shard_map/ppermute | solution.py:210
  183.3 40.4 %collective-permute-start.8 = (bf16[2,256,256]{2,1,0:T(8,128)(2,1)S(1)}, bf16[2,256,256]{2,1,0:T(8,128)(2,1)S(1)}, u32[]{:S(2)}, u32[]{:S(2)}) collective-permute-start(bf16[2,256,256]{2,1,0:T(8,128)(2,1)S(1)} %slice.192), channel_id=1, source_target_pairs={{0,220},{4,224},{8,228},{12,232},{16,236},{20,240},{24,244},{28,24... | collective-permute-start | bytes 786440 | tf_op jit(solution)/shard_map/ppermute | solution.py:210
  233.8 22.4 %collective-permute-start.9 = (bf16[2,512,256]{2,1,0:T(8,128)(2,1)S(1)}, bf16[2,512,256]{2,1,0:T(8,128)(2,1)S(1)}, u32[]{:S(2)}, u32[]{:S(2)}) collective-permute-start(bf16[2,512,256]{2,1,0:T(8,128)(2,1)S(1)} %get-tuple-element.90), channel_id=1, source_target_pairs={{0,4},{4,8},{8,12},{12,16},{16,20},{20,24},{24,28},{28,32},{32,36}... | collective-permute-start | bytes 1572872 | tf_op jit(solution)/shard_map/ppermute | solution.py:210
  233.8 22.6 %collective-permute-start.10 = (bf16[2,256,512]{2,1,0:T(8,128)(2,1)S(1)}, bf16[2,256,512]{2,1,0:T(8,128)(2,1)S(1)}, u32[]{:S(2)}, u32[]{:S(2)}) collective-permute-start(bf16[2,256,512]{2,1,0:T(8,128)(2,1)S(1)} %get-tuple-element.91), channel_id=1, source_target_pairs={{0,32},{4,36},{8,40},{12,44},{16,48},{20,52},{24,56},{28,60},{32,6... | collective-permute-start | bytes 1572872 | tf_op jit(solution)/shard_map/ppermute | solution.py:210
  233.9 22.9 %collective-permute-start.11 = (bf16[2,256,256]{2,1,0:T(8,128)(2,1)S(1)}, bf16[2,256,256]{2,1,0:T(8,128)(2,1)S(1)}, u32[]{:S(2)}, u32[]{:S(2)}) collective-permute-start(bf16[2,256,256]{2,1,0:T(8,128)(2,1)S(1)} %get-tuple-element.92), channel_id=1, source_target_pairs={{0,36},{4,40},{8,44},{12,48},{16,52},{20,56},{24,60},{28,64},{32,6... | collective-permute-start | bytes 786440 | tf_op jit(solution)/shard_map/ppermute | solution.py:210
  256.9 81.4 %copy-start.2 = (f32[2,512,512]{2,1,0:T(8,128)S(1)}, f32[2,512,512]{2,1,0:T(8,128)}, u32[]{:S(2)}) copy-start(f32[2,512,512]{2,1,0:T(8,128)} %copy-done.1) | copy-start | bytes 6291460
Sparse Core Ops, SparseCore 0:
  96.4 81.0 all-reduce.2
  258.1 80.0 all-reduce.4

commit v2 on v1

--- a/solution.py
+++ b/solution.py
@@ -15,6 +15,9 @@
 LANES = 128
 SUBLANES = 8
 CHUNK = 32
+BAND = 3
+RIGHT, LOWER, DIAG, PIECES = 0, 2, 4, 5
+MESH = pl.DeviceIdType.MESH
 
 
 def tables(extent):
@@ -30,8 +33,8 @@
 
 
 def slots_kernel(
-    corners, counts, tile, right, lower, diag, probe, patterns, first, second,
-    grad_tile, grad_right, grad_lower, grad_diag,
+    corners, counts, tile, halo, probe, patterns, first, second,
+    grad_blocks,
     image, grad, padded, rolled, wave, half, spectrum,
 ):
     extent = probe.shape[1]
@@ -43,13 +46,13 @@
         for b in range(own):
             cols = slice(b * LANES, (b + 1) * LANES)
             image[b, ch, :edge] = tile[ch, :, cols]
-            image[b, ch, edge:] = lower[ch, :, cols].astype(f32)
+            inner = slice(b % margin * LANES, (b % margin + 1) * LANES)
+            image[b, ch, edge:] = halo[ch, LOWER + b // margin, :, inner].astype(f32)
         for b in range(margin):
             cols = slice(b * LANES, (b + 1) * LANES)
-            image[own + b, ch, :edge] = right[ch, :, cols].astype(f32)
-            image[own + b, ch, edge:] = diag[ch, :, cols].astype(f32)
-        for b in range(margin):
-            cols = slice(b * LANES, (b + 1) * LANES)
+            for i in range(edge // extent):
+                image[own + b, ch, i * extent:(i + 1) * extent] = halo[ch, RIGHT + i, :, cols].astype(f32)
+            image[own + b, ch, edge:] = halo[ch, DIAG, :, cols].astype(f32)
             padded[ch, b, :SUBLANES] = probe[ch, extent - SUBLANES:, cols]
             padded[ch, b, SUBLANES:] = probe[ch, :, cols]
     grad[...] = jnp.zeros_like(grad)
@@ -161,17 +164,16 @@
     lax.fori_loop(0, counts[0], slot, 0)
 
     for ch in range(2):
-        for b in range(own):
-            cols = slice(b * LANES, (b + 1) * LANES)
-            grad_tile[ch, :, cols] = grad[b, ch, :edge].astype(jnp.bfloat16)
-            grad_lower[ch, :, cols] = grad[b, ch, edge:].astype(jnp.bfloat16)
-        for b in range(margin):
-            cols = slice(b * LANES, (b + 1) * LANES)
-            grad_right[ch, :, cols] = grad[own + b, ch, :edge].astype(jnp.bfloat16)
-            grad_diag[ch, :, cols] = grad[own + b, ch, edge:].astype(jnp.bfloat16)
-
-
-def slot_gradients(tile, right, lower, diag, probe, patterns, corners, counts, first, second):
+        for i in range(BAND):
+            rows = slice(i * extent, (i + 1) * extent)
+            for b in range(BAND * margin):
+                cols = slice(b % margin * LANES, (b % margin + 1) * LANES)
+                grad_blocks[ch, i * BAND + b // margin, :, cols] = grad[b, ch, rows].astype(
+                    jnp.bfloat16
+                )
+
+
+def slot_gradients(tile, halo, probe, patterns, corners, counts, first, second):
     extent = probe.shape[1]
     edge = tile.shape[1]
     total = edge + extent
@@ -181,14 +183,9 @@
     smem = pl.BlockSpec(memory_space=pltpu.SMEM)
     return pl.pallas_call(
         slots_kernel,
-        out_shape=(
-            jax.ShapeDtypeStruct((2, edge, edge), bf16),
-            jax.ShapeDtypeStruct((2, edge, extent), bf16),
-            jax.ShapeDtypeStruct((2, extent, edge), bf16),
-            jax.ShapeDtypeStruct((2, extent, extent), bf16),
-        ),
-        in_specs=[smem, smem] + [vmem] * 8,
-        out_specs=(vmem,) * 4,
+        out_shape=jax.ShapeDtypeStruct((2, BAND * BAND, extent, extent), bf16),
+        in_specs=[smem, smem] + [vmem] * 6,
+        out_specs=vmem,
         scratch_shapes=[
             pltpu.VMEM((blocks, 2, total, LANES), f32),
             pltpu.VMEM((blocks, 2, total, LANES), f32),
@@ -202,37 +199,233 @@
         cost_estimate=pl.CostEstimate(
             flops=4 * 4 * 2 * extent**3 * 2, bytes_accessed=8 * 2**20, transcendentals=0
         ),
-    )(corners, counts, tile, right, lower, diag, probe, patterns, first, second)
-
-
-def shifted_by(value, steps):
-    count = lax.axis_size("tile")
-    return lax.ppermute(value, "tile", [(s, (s + steps) % count) for s in range(count)])
+    )(corners, counts, tile, halo, probe, patterns, first, second)
+
+
+class Place:
+    def __init__(self):
+        self.tiles = lax.axis_size("tile")
+        self.chips = self.tiles * (lax.axis_size("pos") // 2)
+        pos = lax.axis_index("pos")
+        self.core = lax.rem(pos, 2)
+        self.other = 1 - self.core
+        self.flat = lax.div(pos, 2) * self.tiles + lax.axis_index("tile")
+
+    def device(self, steps, core):
+        flat = lax.rem(self.flat + steps + self.chips, self.chips)
+        return lax.rem(flat, self.tiles), lax.div(flat, self.tiles) * 2 + core
+
+    def sibling(self):
+        return self.device(0, self.other)
+
+    def chip(self, steps):
+        return self.device(steps, self.core)
+
+
+def greet(devices):
+    barrier = pltpu.get_barrier_semaphore()
+    for device in devices:
+        pl.semaphore_signal(barrier, inc=1, device_id=device, device_id_type=MESH)
+    pl.semaphore_wait(barrier, len(devices))
+
+
+def halo_targets(i, j):
+    targets = []
+    if j == 0:
+        targets.append((RIGHT + i, -1))
+    if i == 0:
+        targets.append((LOWER + j, -TILE_COLS))
+    if i == 0 and j == 0:
+        targets.append((DIAG, -TILE_COLS - 1))
+    return targets
+
+
+def remote(source, target, sems, at, device):
+    return pltpu.make_async_remote_copy(
+        src_ref=source,
+        dst_ref=target,
+        send_sem=sems.at[0, at],
+        recv_sem=sems.at[1, at],
+        device_id=device,
+        device_id_type=MESH,
+    )
+
+
+def block_of(ref, channel, i, j, extent):
+    return ref.at[channel, i * extent:(i + 1) * extent, j * extent:(j + 1) * extent]
+
+
+def first_halo_kernel(tile, halo, outgoing, halo_sems, pass_sems):
+    place = Place()
+    extent = outgoing.shape[-1]
+    core = place.core
+    greet(
+        [place.sibling()]
+        + [place.chip(sign * s) for s in (1, TILE_COLS, TILE_COLS + 1) for sign in (1, -1)]
+    )
+    copies = {}
+    for i, j in ((0, 0), (1, 0), (0, 1)):
+        outgoing[2 * i + j] = block_of(tile, core, i, j, extent)[...].astype(jnp.bfloat16)
+        for piece, steps in halo_targets(i, j):
+            copies[piece] = remote(
+                outgoing.at[2 * i + j], halo.at[core, piece], halo_sems, piece, place.chip(steps)
+            )
+            copies[piece].start()
+    finish_halo(place, halo, copies, pass_sems)
+
+
+def finish_halo(place, halo, copies, pass_sems):
+    passes = []
+    for piece, copy in copies.items():
+        copy.wait_recv()
+        mine = halo.at[place.core, piece]
+        passes.append(remote(mine, mine, pass_sems, piece, place.sibling()))
+        passes[-1].start()
+    for copy in passes:
+        copy.wait()
+    for copy in copies.values():
+        copy.wait_send()
+
+
+def reduce_kernel(
+    last, grads, tile, refined, *rest,
+):
+    (halo, outgoing, halo_sems, pass_sems) = rest[:4] if not last else (None,) * 4
+    (pair, edges, edges_in, sums, sums_in, totals, totals_in,
+     pair_sems, edge_sems, sum_sems, total_sems) = rest[0 if last else 4:]
+    place = Place()
+    extent = grads.shape[-1]
+    core, other = place.core, place.other
+    f32, bf16 = jnp.float32, jnp.bfloat16
+    across = place.tiles
+    greet(
+        [place.sibling(), place.chip(across)]
+        + [place.chip(sign * s) for s in (1, TILE_COLS, TILE_COLS + 1) for sign in (1, -1)]
+    )
+    margins = {5: (1, 1), 7: (3, TILE_COLS), 2: (0, 1), 8: (4, TILE_COLS + 1), 6: (2, TILE_COLS)}
+    order = ((1, 1), (1, 0), (0, 0), (0, 1))
+    needs = {(1, 1): (), (1, 0): (1,), (0, 0): (0, 2, 4), (0, 1): (3,)}
+    pair_copies = {}
+    for k in [4, *margins, 3, 0, 1]:
+        pair_copies[k] = remote(grads.at[other, k], pair.at[k], pair_sems, k, place.sibling())
+        pair_copies[k].start()
+    edge_copies = {}
+    sum_copies = {}
+
+    def send_sum(i, j):
+        k = BAND * i + j
+        at = 2 * i + j
+        pair_copies[k].wait_recv()
+        value = grads[core, k].astype(f32) + pair[k].astype(f32)
+        for m in needs[i, j]:
+            edge_copies[m].wait_recv()
+            value = value + edges_in[m].astype(f32)
+        sums[at] = value.astype(bf16)
+        sum_copies[at] = remote(sums.at[at], sums_in.at[at], sum_sems, at, place.chip(across))
+        sum_copies[at].start()
+
+    send_sum(1, 1)
+    for k, (m, steps) in margins.items():
+        pair_copies[k].wait_recv()
+        edges[m] = (grads[core, k].astype(f32) + pair[k].astype(f32)).astype(bf16)
+        edge_copies[m] = remote(edges.at[m], edges_in.at[m], edge_sems, m, place.chip(steps))
+        edge_copies[m].start()
+    for i, j in order[1:]:
+        send_sum(i, j)
+
+    total_copies = {}
+    halo_copies = {}
+    for i, j in order:
+        at = 2 * i + j
+        sum_copies[at].wait_recv()
+        total = (sums[at].astype(f32) + sums_in[at].astype(f32)).astype(bf16)
+        totals[at] = total
+        total_copies[at] = remote(
+            totals.at[at], totals_in.at[at], total_sems, at, place.sibling()
+        )
+        total_copies[at].start()
+        fresh = block_of(tile, core, i, j, extent)[...] - LEARNING_RATE * total.astype(f32)
+        block_of(refined, core, i, j, extent)[...] = fresh
+        if not last and (i, j) != (1, 1):
+            outgoing[at] = fresh.astype(bf16)
+            for piece, steps in halo_targets(i, j):
+                halo_copies[piece] = remote(
+                    outgoing.at[at], halo.at[core, piece], halo_sems, piece, place.chip(steps)
+                )
+                halo_copies[piece].start()
+    for i, j in order:
+        at = 2 * i + j
+        total_copies[at].wait_recv()
+        block_of(refined, other, i, j, extent)[...] = block_of(tile, other, i, j, extent)[
+            ...
+        ] - LEARNING_RATE * totals_in[at].astype(f32)
+    if not last:
+        finish_halo(place, halo, halo_copies, pass_sems)
+    for group in (pair_copies, edge_copies, sum_copies, total_copies):
+        for copy in group.values():
+            copy.wait_send()
+
+
+def sems(count):
+    return pltpu.SemaphoreType.DMA((2, count))
+
+
+def first_halo(tile, extent):
+    vmem = pl.BlockSpec(memory_space=pltpu.VMEM)
+    return pl.pallas_call(
+        first_halo_kernel,
+        out_shape=jax.ShapeDtypeStruct((2, PIECES, extent, extent), jnp.bfloat16),
+        in_specs=[vmem],
+        out_specs=vmem,
+        scratch_shapes=[
+            pltpu.VMEM((4, extent, extent), jnp.bfloat16),
+            sems(PIECES),
+            sems(PIECES),
+        ],
+        compiler_params=pltpu.CompilerParams(
+            collective_id=0, has_side_effects=True, vmem_limit_bytes=40 * 1024 * 1024
+        ),
+    )(tile)
+
+
+def reduce_and_update(grads, tile, last):
+    extent = grads.shape[-1]
+    vmem = pl.BlockSpec(memory_space=pltpu.VMEM)
+
+    def blocks(count):
+        return pltpu.VMEM((count, extent, extent), jnp.bfloat16)
+
+    shapes = [jax.ShapeDtypeStruct(tile.shape, tile.dtype)]
+    scratch = []
+    if not last:
+        shapes.append(jax.ShapeDtypeStruct((2, PIECES, extent, extent), jnp.bfloat16))
+        scratch += [blocks(4), sems(PIECES), sems(PIECES)]
+    scratch += [blocks(BAND * BAND), blocks(PIECES), blocks(PIECES), blocks(4), blocks(4)]
+    scratch += [blocks(4), blocks(4), sems(BAND * BAND), sems(PIECES), sems(4), sems(4)]
+    return pl.pallas_call(
+        functools.partial(reduce_kernel, last),
+        out_shape=tuple(shapes),
+        in_specs=[vmem, vmem],
+        out_specs=(vmem,) * len(shapes),
+        scratch_shapes=scratch,
+        compiler_params=pltpu.CompilerParams(
+            collective_id=2 if last else 1,
+            has_side_effects=True,
+            vmem_limit_bytes=40 * 1024 * 1024,
+        ),
+    )(grads, tile)
 
 
 def shards(object_tiles, probe, patterns, corners, counts):
     tile = object_tiles[0]
     extent = probe.shape[1]
     first, second = tables(extent)
+    halo = first_halo(tile, extent)
     for repeat in range(ITERS):
-        short = tile.astype(jnp.bfloat16)
-        right = shifted_by(short[:, :, :extent], -1)
-        lower = shifted_by(short[:, :extent, :], -TILE_COLS)
-        diag = shifted_by(short[:, :extent, :extent], -TILE_COLS - 1)
-        grads = slot_gradients(
-            tile, right, lower, diag, probe, patterns, corners, counts, first, second
-        )
-        total, *margins = grads
-        total = total.astype(jnp.float32)
-        right_in = shifted_by(margins[0], 1).astype(jnp.float32)
-        lower_in = shifted_by(margins[1], TILE_COLS).astype(jnp.float32)
-        diag_in = shifted_by(margins[2], TILE_COLS + 1).astype(jnp.float32)
-        total = total.at[:, :, :extent].add(right_in)
-        total = total.at[:, :extent, :].add(lower_in)
-        total = total.at[:, :extent, :extent].add(diag_in)
-        tile = tile - LEARNING_RATE * lax.psum(total.astype(jnp.bfloat16), "pos").astype(
-            jnp.float32
-        )
+        grads = slot_gradients(tile, halo, probe, patterns, corners, counts, first, second)
+        tile, *rest = reduce_and_update(grads, tile, repeat == ITERS - 1)
+        if rest:
+            halo = rest[0]
     return tile[None]
 
 

time: 348 us -> 152 us (0.44)
  the two profiles are of different devices: /device:TPU:1 before, /device:TPU:83 now
where the time goes in v2:
time: 152 us
  Pallas kernels  147 us (97%)
  local copies, waits for them, and re-layouts  3.68 us (2%)
    pallas_call x2, Pallas kernels, reduce_and_update(): pl.pallas_call(functools.partial(reduce_kernel, last), out_shape=tuple(sh...  109 us
    pallas_call x2, Pallas kernels, slot_gradients(): pl.pallas_call(slots_kernel, out_shape=jax.ShapeDtypeStruct((2, BAND * BA...  22.4 us
    pallas_call x1, Pallas kernels, first_halo(): pl.pallas_call(first_halo_kernel, out_shape=jax.ShapeDtypeStruct((2, PIEC...  16.4 us
    unnamed x12, local copies, waits for them, and re-layouts  3.68 us

profile of v2, /device:TPU:83, one launch (start us, length us, event | category | flops | bytes accessed | tf_op | source)
XLA Modules:
  0.0 151.9 jit_solution(17123744178007944928)
XLA Ops:
  0.7 0.8 copy.9.corners
  1.4 0.0 copy-start
  1.4 1.6 %copy-done = f32[1,2,512,512]{3,2,1,0:T(8,128)S(1)} copy-done((f32[1,2,512,512]{3,2,1,0:T(8,128)S(1)}, f32[1,2,512,512]{3,2,1,0:T(8,128)}, u32[]{:S(2)}) %copy-start) | copy-done | bytes 2097176
  3.0 0.0 copy-start.1
  3.0 0.0 copy-start.2
  3.0 0.0 copy-start.3
  3.0 0.0 copy-start.4
  3.0 16.4 %shard_map.73.halo = bf16[2,5,256,256]{3,2,1,0:T(8,128)(2,1)S(1)} custom-call(f32[2,512,512]{2,1,0:T(8,128)S(1)} %bitcast.2), custom_call_target="tpu_custom_call" | custom-call | tf_op jit(solution)/shard_map/pallas_call | solution.py:375
  19.4 0.0 copy-done.1
  19.4 0.0 copy-done.2
  19.4 0.0 copy-done.3
  19.4 0.0 copy-done.4
  19.4 11.2 %shard_map.74.grads = bf16[2,9,256,256]{3,2,1,0:T(8,128)(2,1)S(1)} custom-call(s32[8,2]{1,0:T(8,128)S(1)} %copy.9.corners, s32[1]{0:T(128)S(6)} %copy.11.counts, f32[2,512,512]{2,1,0:T(8,128)S(1)} %bitcast.3, bf16[2,5,256,256]{3,2,1,0:T(8,128)(2,1)S(1)} %shard_map.73.halo, f32[2,256,256]{2,1,0:T(8,128)S(1)} %copy-done.2, bf16[8,256,256]{2,1,0:T(8,128)(2,1)S(1)} %copy-done.1, ...), custom_call_target="tpu_custom_call" | custom-call | flops 1073741824 | bytes 8388608 | tf_op jit(solution)/shard_map/pallas_call | solution.py:184
  30.7 64.5 %shard_map.75 = (f32[2,512,512]{2,1,0:T(8,128)S(1)}, bf16[2,5,256,256]{3,2,1,0:T(8,128)(2,1)S(1)}) custom-call(bf16[2,9,256,256]{3,2,1,0:T(8,128)(2,1)S(1)} %shard_map.74.grads, f32[2,512,512]{2,1,0:T(8,128)S(1)} %bitcast.4), custom_call_target="tpu_custom_call" | custom-call | tf_op jit(solution)/shard_map/pallas_call | solution.py:405
  95.1 11.2 %shard_map.76.grads = bf16[2,9,256,256]{3,2,1,0:T(8,128)(2,1)S(1)} custom-call(s32[8,2]{1,0:T(8,128)S(1)} %copy.9.corners, s32[1]{0:T(128)S(6)} %copy.11.counts, f32[2,512,512]{2,1,0:T(8,128)S(1)} %get-tuple-element.7.tile, bf16[2,5,256,256]{3,2,1,0:T(8,128)(2,1)S(1)} %get-tuple-element.8.halo, f32[2,256,256]{2,1,0:T(8,128)S(1)} %copy-done.2, ...), custom_call_target="tpu_custom_call" | custom-call | flops 1073741824 | bytes 8388608 | tf_op jit(solution)/shard_map/pallas_call | solution.py:184
  106.3 44.2 %shard_map.77 = f32[2,512,512]{2,1,0:T(8,128)S(1)} custom-call(bf16[2,9,256,256]{3,2,1,0:T(8,128)(2,1)S(1)} %shard_map.76.grads, f32[2,512,512]{2,1,0:T(8,128)S(1)} %get-tuple-element.7.tile), custom_call_target="tpu_custom_call" | custom-call | tf_op jit(solution)/shard_map/pallas_call | solution.py:405
  150.5 1.3 copy.12
Async XLA Ops:
  1.4 1.6 %copy-start = (f32[1,2,512,512]{3,2,1,0:T(8,128)S(1)}, f32[1,2,512,512]{3,2,1,0:T(8,128)}, u32[]{:S(2)}) copy-start(f32[1,2,512,512]{3,2,1,0:T(8,128)} %param.7) | copy-start | bytes 6291460
  3.0 16.4 %copy-start.1 = (bf16[8,256,256]{2,1,0:T(8,128)(2,1)S(1)}, bf16[8,256,256]{2,1,0:T(8,128)(2,1)}, u32[]{:S(2)}) copy-start(bf16[8,256,256]{2,1,0:T(8,128)(2,1)} %patterns.3) | copy-start | bytes 3145732
  3.0 16.4 %copy-start.2 = (f32[2,256,256]{2,1,0:T(8,128)S(1)}, f32[2,256,256]{2,1,0:T(8,128)}, u32[]{:S(2)}) copy-start(f32[2,256,256]{2,1,0:T(8,128)} %probe.3) | copy-start | bytes 1572868
  3.0 16.4 %copy-start.3 = (bf16[512,512]{1,0:T(8,128)(2,1)S(1)}, bf16[512,512]{1,0:T(8,128)(2,1)}, u32[]{:S(2)}) copy-start(bf16[512,512]{1,0:T(8,128)(2,1)} %constant.5.clone.second) | copy-start | bytes 1572868
  3.0 16.4 %copy-start.4 = (bf16[512,512]{1,0:T(8,128)(2,1)S(1)}, bf16[512,512]{1,0:T(8,128)(2,1)}, u32[]{:S(2)}) copy-start(bf16[512,512]{1,0:T(8,128)(2,1)} %constant.4.clone.first) | copy-start | bytes 1572868

commit v3 on v2

--- a/solution.py
+++ b/solution.py
@@ -17,6 +17,7 @@
 CHUNK = 32
 BAND = 3
 RIGHT, LOWER, DIAG, PIECES = 0, 2, 4, 5
+PLANE = 16
 MESH = pl.DeviceIdType.MESH
 
 
@@ -210,10 +211,13 @@
         self.core = lax.rem(pos, 2)
         self.other = 1 - self.core
         self.flat = lax.div(pos, 2) * self.tiles + lax.axis_index("tile")
+        self.local = lax.rem(self.flat, PLANE)
+
+    def at(self, flat, core):
+        return lax.rem(flat, self.tiles), lax.div(flat, self.tiles) * 2 + core
 
     def device(self, steps, core):
-        flat = lax.rem(self.flat + steps + self.chips, self.chips)
-        return lax.rem(flat, self.tiles), lax.div(flat, self.tiles) * 2 + core
+        return self.at(lax.rem(self.flat + steps + self.chips, self.chips), core)
 
     def sibling(self):
         return self.device(0, self.other)
@@ -221,8 +225,20 @@
     def chip(self, steps):
         return self.device(steps, self.core)
 
-
-def greet(devices):
+    def in_plane(self, steps):
+        local = lax.rem(self.local + steps + PLANE, PLANE)
+        return self.at(self.flat - self.local + local, self.core)
+
+    def leaves(self, steps):
+        ends = self.local + steps
+        return jnp.logical_and(self.core == 1, jnp.logical_or(ends < 0, ends >= PLANE))
+
+
+def greet(place, extra=()):
+    devices = [place.sibling(), place.chip(PLANE), place.chip(-PLANE), *extra]
+    for steps in (1, TILE_COLS, TILE_COLS + 1):
+        for sign in (1, -1):
+            devices += [place.chip(sign * steps), place.in_plane(sign * steps)]
     barrier = pltpu.get_barrier_semaphore()
     for device in devices:
         pl.semaphore_signal(barrier, inc=1, device_id=device, device_id_type=MESH)
@@ -251,33 +267,73 @@
     )
 
 
+class Routed:
+    def __init__(self, place, steps, source, target, via, at, direct_sems, via_sems, on_sems):
+        self.direct = remote(source, target, direct_sems, at, place.chip(steps))
+        self.away = remote(source, via.at[at], via_sems, at, place.in_plane(steps))
+        self.onward = pltpu.make_async_remote_copy(
+            src_ref=via.at[at],
+            dst_ref=target,
+            send_sem=on_sems.at[at],
+            recv_sem=direct_sems.at[1, at],
+            device_id=place.chip(PLANE if steps > 0 else -PLANE),
+            device_id_type=MESH,
+        )
+        self.leaves = place.leaves(steps)
+        self.hands_on = place.leaves(-steps)
+
+    def start(self):
+        @pl.when(self.leaves)
+        def _():
+            self.away.start()
+
+        @pl.when(jnp.logical_not(self.leaves))
+        def _():
+            self.direct.start()
+
+    def hand_on(self):
+        @pl.when(self.hands_on)
+        def _():
+            self.away.wait_recv()
+            self.onward.start()
+
+    def wait_recv(self):
+        self.direct.wait_recv()
+
+    def wait_send(self):
+        @pl.when(self.leaves)
+        def _():
+            self.away.wait_send()
+
+        @pl.when(jnp.logical_not(self.leaves))
+        def _():
+            self.direct.wait_send()
+
+        @pl.when(self.hands_on)
+        def _():
+            self.onward.wait_send()
+
+
 def block_of(ref, channel, i, j, extent):
     return ref.at[channel, i * extent:(i + 1) * extent, j * extent:(j + 1) * extent]
 
 
-def first_halo_kernel(tile, halo, outgoing, halo_sems, pass_sems):
-    place = Place()
-    extent = outgoing.shape[-1]
-    core = place.core
-    greet(
-        [place.sibling()]
-        + [place.chip(sign * s) for s in (1, TILE_COLS, TILE_COLS + 1) for sign in (1, -1)]
-    )
-    copies = {}
-    for i, j in ((0, 0), (1, 0), (0, 1)):
-        outgoing[2 * i + j] = block_of(tile, core, i, j, extent)[...].astype(jnp.bfloat16)
-        for piece, steps in halo_targets(i, j):
-            copies[piece] = remote(
-                outgoing.at[2 * i + j], halo.at[core, piece], halo_sems, piece, place.chip(steps)
-            )
-            copies[piece].start()
-    finish_halo(place, halo, copies, pass_sems)
-
-
-def finish_halo(place, halo, copies, pass_sems):
+HALO_ORDER = (RIGHT + 1, RIGHT, LOWER, DIAG, LOWER + 1)
+
+
+def send_halos(place, copies, i, j, outgoing, halo, via, halo_sems, via_sems, on_sems):
+    for piece, steps in halo_targets(i, j):
+        copies[piece] = Routed(
+            place, steps, outgoing.at[2 * i + j], halo.at[place.core, piece], via, piece,
+            halo_sems, via_sems, on_sems,
+        )
+        copies[piece].start()
+
+
+def pass_halos(place, halo, copies, pass_sems):
     passes = []
-    for piece, copy in copies.items():
-        copy.wait_recv()
+    for piece in HALO_ORDER:
+        copies[piece].wait_recv()
         mine = halo.at[place.core, piece]
         passes.append(remote(mine, mine, pass_sems, piece, place.sibling()))
         passes[-1].start()
@@ -287,21 +343,31 @@
         copy.wait_send()
 
 
-def reduce_kernel(
-    last, grads, tile, refined, *rest,
-):
-    (halo, outgoing, halo_sems, pass_sems) = rest[:4] if not last else (None,) * 4
-    (pair, edges, edges_in, sums, sums_in, totals, totals_in,
-     pair_sems, edge_sems, sum_sems, total_sems) = rest[0 if last else 4:]
+def first_halo_kernel(tile, halo, outgoing, via, halo_sems, via_sems, on_sems, pass_sems):
+    place = Place()
+    extent = outgoing.shape[-1]
+    greet(place)
+    copies = {}
+    for i, j in ((1, 0), (0, 0), (0, 1)):
+        outgoing[2 * i + j] = block_of(tile, place.core, i, j, extent)[...].astype(jnp.bfloat16)
+        send_halos(place, copies, i, j, outgoing, halo, via, halo_sems, via_sems, on_sems)
+    for piece in HALO_ORDER:
+        copies[piece].hand_on()
+    pass_halos(place, halo, copies, pass_sems)
+
+
+def reduce_kernel(last, grads, tile, refined, *rest):
+    if not last:
+        halo, outgoing, halo_via, halo_sems, halo_via_sems, halo_on_sems, pass_sems = rest[:7]
+        rest = rest[7:]
+    (pair, edges, edges_in, edges_via, sums, sums_in, totals, totals_in,
+     pair_sems, edge_sems, edge_via_sems, edge_on_sems, sum_sems, total_sems) = rest
     place = Place()
     extent = grads.shape[-1]
     core, other = place.core, place.other
     f32, bf16 = jnp.float32, jnp.bfloat16
     across = place.tiles
-    greet(
-        [place.sibling(), place.chip(across)]
-        + [place.chip(sign * s) for s in (1, TILE_COLS, TILE_COLS + 1) for sign in (1, -1)]
-    )
+    greet(place, (place.chip(across),))
     margins = {5: (1, 1), 7: (3, TILE_COLS), 2: (0, 1), 8: (4, TILE_COLS + 1), 6: (2, TILE_COLS)}
     order = ((1, 1), (1, 0), (0, 0), (0, 1))
     needs = {(1, 1): (), (1, 0): (1,), (0, 0): (0, 2, 4), (0, 1): (3,)}
@@ -328,10 +394,17 @@
     for k, (m, steps) in margins.items():
         pair_copies[k].wait_recv()
         edges[m] = (grads[core, k].astype(f32) + pair[k].astype(f32)).astype(bf16)
-        edge_copies[m] = remote(edges.at[m], edges_in.at[m], edge_sems, m, place.chip(steps))
+        edge_copies[m] = Routed(
+            place, steps, edges.at[m], edges_in.at[m], edges_via, m,
+            edge_sems, edge_via_sems, edge_on_sems,
+        )
         edge_copies[m].start()
-    for i, j in order[1:]:
-        send_sum(i, j)
+    edge_copies[1].hand_on()
+    send_sum(1, 0)
+    for m in (3, 0, 4, 2):
+        edge_copies[m].hand_on()
+    send_sum(0, 0)
+    send_sum(0, 1)
 
     total_copies = {}
     halo_copies = {}
@@ -348,11 +421,15 @@
         block_of(refined, core, i, j, extent)[...] = fresh
         if not last and (i, j) != (1, 1):
             outgoing[at] = fresh.astype(bf16)
-            for piece, steps in halo_targets(i, j):
-                halo_copies[piece] = remote(
-                    outgoing.at[at], halo.at[core, piece], halo_sems, piece, place.chip(steps)
-                )
-                halo_copies[piece].start()
+            send_halos(
+                place, halo_copies, i, j, outgoing, halo, halo_via,
+                halo_sems, halo_via_sems, halo_on_sems,
+            )
+            if (i, j) == (0, 0):
+                halo_copies[RIGHT + 1].hand_on()
+    if not last:
+        for piece in HALO_ORDER[1:]:
+            halo_copies[piece].hand_on()
     for i, j in order:
         at = 2 * i + j
         total_copies[at].wait_recv()
@@ -360,7 +437,7 @@
             ...
         ] - LEARNING_RATE * totals_in[at].astype(f32)
     if not last:
-        finish_halo(place, halo, halo_copies, pass_sems)
+        pass_halos(place, halo, halo_copies, pass_sems)
     for group in (pair_copies, edge_copies, sum_copies, total_copies):
         for copy in group.values():
             copy.wait_send()
@@ -379,7 +456,10 @@
         out_specs=vmem,
         scratch_shapes=[
             pltpu.VMEM((4, extent, extent), jnp.bfloat16),
+            pltpu.VMEM((PIECES, extent, extent), jnp.bfloat16),
             sems(PIECES),
+            sems(PIECES),
+            pltpu.SemaphoreType.DMA((PIECES,)),
             sems(PIECES),
         ],
         compiler_params=pltpu.CompilerParams(
@@ -395,13 +475,15 @@
     def blocks(count):
         return pltpu.VMEM((count, extent, extent), jnp.bfloat16)
 
+    onward = pltpu.SemaphoreType.DMA((PIECES,))
     shapes = [jax.ShapeDtypeStruct(tile.shape, tile.dtype)]
     scratch = []
     if not last:
         shapes.append(jax.ShapeDtypeStruct((2, PIECES, extent, extent), jnp.bfloat16))
-        scratch += [blocks(4), sems(PIECES), sems(PIECES)]
-    scratch += [blocks(BAND * BAND), blocks(PIECES), blocks(PIECES), blocks(4), blocks(4)]
-    scratch += [blocks(4), blocks(4), sems(BAND * BAND), sems(PIECES), sems(4), sems(4)]
+        scratch += [blocks(4), blocks(PIECES), sems(PIECES), sems(PIECES), onward, sems(PIECES)]
+    scratch += [blocks(BAND * BAND), blocks(PIECES), blocks(PIECES), blocks(PIECES)]
+    scratch += [blocks(4), blocks(4), blocks(4), blocks(4)]
+    scratch += [sems(BAND * BAND), sems(PIECES), sems(PIECES), onward, sems(4), sems(4)]
     return pl.pallas_call(
         functools.partial(reduce_kernel, last),
         out_shape=tuple(shapes),

time: 152 us -> 155 us (1.020)
  the two profiles are of different devices: /device:TPU:83 before, /device:TPU:1 now
where the time goes in v3:
time: 155 us; the launch traced here: 154 us
  Pallas kernels  150 us (97%)
  local copies, waits for them, and re-layouts  3.68 us (2%)
    pallas_call x2, Pallas kernels, reduce_and_update(): pl.pallas_call(functools.partial(reduce_kernel, last), out_shape=tuple(sh...  119 us
    pallas_call x1, Pallas kernels, first_halo(): pl.pallas_call(first_halo_kernel, out_shape=jax.ShapeDtypeStruct((2, PIEC...  22.3 us
    pallas_call x2, Pallas kernels, slot_gradients(): pl.pallas_call(slots_kernel, out_shape=jax.ShapeDtypeStruct((2, BAND * BA...  8.52 us
    unnamed x12, local copies, waits for them, and re-layouts  3.68 us

profile of v3, /device:TPU:1, one launch (start us, length us, event | category | flops | bytes accessed | tf_op | source)
XLA Modules:
  0.0 154.3 jit_solution(8104907713453176581)
XLA Ops:
  0.7 0.8 copy.9.corners
  1.4 0.0 copy-start
  1.4 1.6 %copy-done = f32[1,2,512,512]{3,2,1,0:T(8,128)S(1)} copy-done((f32[1,2,512,512]{3,2,1,0:T(8,128)S(1)}, f32[1,2,512,512]{3,2,1,0:T(8,128)}, u32[]{:S(2)}) %copy-start) | copy-done | bytes 2097176
  3.0 0.0 copy-start.1
  3.0 0.0 copy-start.2
  3.0 0.0 copy-start.3
  3.0 0.0 copy-start.4
  3.0 22.3 %shard_map.73.halo = bf16[2,5,256,256]{3,2,1,0:T(8,128)(2,1)S(1)} custom-call(f32[2,512,512]{2,1,0:T(8,128)S(1)} %bitcast.2), custom_call_target="tpu_custom_call" | custom-call | tf_op jit(solution)/shard_map/pallas_call | solution.py:452
  25.3 0.0 copy-done.1
  25.3 0.0 copy-done.2
  25.3 0.0 copy-done.3
  25.3 0.0 copy-done.4
  25.3 4.3 %shard_map.74.grads = bf16[2,9,256,256]{3,2,1,0:T(8,128)(2,1)S(1)} custom-call(s32[8,2]{1,0:T(8,128)S(1)} %copy.9.corners, s32[1]{0:T(128)S(6)} %copy.11.counts, f32[2,512,512]{2,1,0:T(8,128)S(1)} %bitcast.3, bf16[2,5,256,256]{3,2,1,0:T(8,128)(2,1)S(1)} %shard_map.73.halo, f32[2,256,256]{2,1,0:T(8,128)S(1)} %copy-done.2, bf16[8,256,256]{2,1,0:T(8,128)(2,1)S(1)} %copy-done.1, ...), custom_call_target="tpu_custom_call" | custom-call | flops 1073741824 | bytes 8388608 | tf_op jit(solution)/shard_map/pallas_call | solution.py:185
  29.6 61.7 %shard_map.75 = (f32[2,512,512]{2,1,0:T(8,128)S(1)}, bf16[2,5,256,256]{3,2,1,0:T(8,128)(2,1)S(1)}) custom-call(bf16[2,9,256,256]{3,2,1,0:T(8,128)(2,1)S(1)} %shard_map.74.grads, f32[2,512,512]{2,1,0:T(8,128)S(1)} %bitcast.4), custom_call_target="tpu_custom_call" | custom-call | tf_op jit(solution)/shard_map/pallas_call | solution.py:487
  91.3 4.3 %shard_map.76.grads = bf16[2,9,256,256]{3,2,1,0:T(8,128)(2,1)S(1)} custom-call(s32[8,2]{1,0:T(8,128)S(1)} %copy.9.corners, s32[1]{0:T(128)S(6)} %copy.11.counts, f32[2,512,512]{2,1,0:T(8,128)S(1)} %get-tuple-element.7.tile, bf16[2,5,256,256]{3,2,1,0:T(8,128)(2,1)S(1)} %get-tuple-element.8.halo, f32[2,256,256]{2,1,0:T(8,128)S(1)} %copy-done.2, ...), custom_call_target="tpu_custom_call" | custom-call | flops 1073741824 | bytes 8388608 | tf_op jit(solution)/shard_map/pallas_call | solution.py:185
  95.6 57.4 %shard_map.77 = f32[2,512,512]{2,1,0:T(8,128)S(1)} custom-call(bf16[2,9,256,256]{3,2,1,0:T(8,128)(2,1)S(1)} %shard_map.76.grads, f32[2,512,512]{2,1,0:T(8,128)S(1)} %get-tuple-element.7.tile), custom_call_target="tpu_custom_call" | custom-call | tf_op jit(solution)/shard_map/pallas_call | solution.py:487
  153.0 1.3 copy.12
Async XLA Ops:
  1.4 1.6 %copy-start = (f32[1,2,512,512]{3,2,1,0:T(8,128)S(1)}, f32[1,2,512,512]{3,2,1,0:T(8,128)}, u32[]{:S(2)}) copy-start(f32[1,2,512,512]{3,2,1,0:T(8,128)} %param.7) | copy-start | bytes 6291460
  3.0 22.3 %copy-start.1 = (bf16[8,256,256]{2,1,0:T(8,128)(2,1)S(1)}, bf16[8,256,256]{2,1,0:T(8,128)(2,1)}, u32[]{:S(2)}) copy-start(bf16[8,256,256]{2,1,0:T(8,128)(2,1)} %patterns.3) | copy-start | bytes 3145732
  3.0 22.3 %copy-start.2 = (f32[2,256,256]{2,1,0:T(8,128)S(1)}, f32[2,256,256]{2,1,0:T(8,128)}, u32[]{:S(2)}) copy-start(f32[2,256,256]{2,1,0:T(8,128)} %probe.3) | copy-start | bytes 1572868
  3.0 22.3 %copy-start.3 = (bf16[512,512]{1,0:T(8,128)(2,1)S(1)}, bf16[512,512]{1,0:T(8,128)(2,1)}, u32[]{:S(2)}) copy-start(bf16[512,512]{1,0:T(8,128)(2,1)} %constant.5.clone.second) | copy-start | bytes 1572868
  3.0 22.3 %copy-start.4 = (bf16[512,512]{1,0:T(8,128)(2,1)S(1)}, bf16[512,512]{1,0:T(8,128)(2,1)}, u32[]{:S(2)}) copy-start(bf16[512,512]{1,0:T(8,128)(2,1)} %constant.4.clone.first) | copy-start | bytes 1572868

commit v4 on v3

--- a/solution.py
+++ b/solution.py
@@ -15,6 +15,7 @@
 LANES = 128
 SUBLANES = 8
 CHUNK = 32
+GROUP = 16
 BAND = 3
 RIGHT, LOWER, DIAG, PIECES = 0, 2, 4, 5
 PLANE = 16
@@ -28,20 +29,31 @@
     factor = 1.0 / math.sqrt(extent)
     cosine = np.cos(angles) * factor
     sine_neg = -np.sin(angles) * factor
-    first = np.block([[cosine, sine_neg], [-sine_neg, cosine]])
-    second = np.block([[cosine, -sine_neg], [sine_neg, cosine]])
-    return jnp.asarray(first, jnp.bfloat16), jnp.asarray(second, jnp.bfloat16)
+    matrices = []
+    for parity in range(2):
+        c = cosine[:extent // 2, parity::2]
+        d = sine_neg[:extent // 2, parity::2]
+        matrices.append(np.block([[c, d], [-d, c]]))
+    matrices += [matrices[0].T, matrices[1].T]
+    rows = np.arange(extent).reshape(2, -1, GROUP).swapaxes(0, 1).reshape(-1)
+    matrices += [matrices[at][rows] for at in range(4)]
+    order = np.concatenate([counter[0::2], counter[1::2]])
+    split = (counter[:, None] == order[None, :]).astype(np.float32)
+    return jnp.asarray(np.stack(matrices), jnp.bfloat16), jnp.asarray(
+        np.stack([split, split.T]), jnp.bfloat16
+    )
 
 
 def slots_kernel(
-    corners, counts, tile, halo, probe, patterns, first, second,
+    corners, counts, tile, halo, probe, patterns, table,
     grad_blocks,
-    image, grad, padded, rolled, wave, half, spectrum,
+    image, grad, padded, rolled, wave, half,
 ):
     extent = probe.shape[1]
     edge = tile.shape[1]
     own = edge // LANES
     margin = extent // LANES
+    mid_row = extent // 2
     f32 = jnp.float32
     for ch in range(2):
         for b in range(own):
@@ -58,111 +70,170 @@
             padded[ch, b, SUBLANES:] = probe[ch, :, cols]
     grad[...] = jnp.zeros_like(grad)
 
-    def slot(g, carry):
-        row = corners[g, 0]
-        col = corners[g, 1]
-        row_off = lax.rem(row, SUBLANES)
-        col_off = lax.rem(col, LANES)
-        row_at = pl.multiple_of(row - row_off, SUBLANES)
-        block = lax.div(col, LANES)
-        lane = lax.broadcasted_iota(jnp.int32, (CHUNK, LANES), 1)
-        keep = lane >= col_off
-        lane8 = lax.broadcasted_iota(jnp.int32, (SUBLANES, LANES), 1)
-        sub8 = lax.broadcasted_iota(jnp.int32, (SUBLANES, LANES), 0)
-        keep8 = lane8 >= col_off
-        stay8 = sub8 >= row_off
-        over = pl.multiple_of(row_at + extent, SUBLANES)
-
-        for i in range(0, extent, CHUNK):
-            here = slice(i, i + CHUNK)
-            shifted = []
-            for ch in range(2):
-                turned = [
-                    pltpu.roll(
-                        padded[ch, b, pl.ds(SUBLANES - row_off + i, CHUNK), :], col_off, 1
+    class Slot:
+        def __init__(self, g, lane):
+            self.g, self.lane = g, lane
+            row, col = corners[g, 0], corners[g, 1]
+            self.row_off = lax.rem(row, SUBLANES)
+            self.col_off = lax.rem(col, LANES)
+            self.row_at = pl.multiple_of(row - self.row_off, SUBLANES)
+            self.block = lax.div(col, LANES)
+            self.keep = lax.broadcasted_iota(jnp.int32, (CHUNK, LANES), 1) >= self.col_off
+            self.keep8 = lax.broadcasted_iota(jnp.int32, (SUBLANES, LANES), 1) >= self.col_off
+            self.stay8 = lax.broadcasted_iota(jnp.int32, (SUBLANES, LANES), 0) >= self.row_off
+            self.below = pl.ds(pl.multiple_of(self.row_at + extent, SUBLANES), SUBLANES)
+
+        def rows(self, i, number=CHUNK):
+            return pl.ds(pl.multiple_of(self.row_at + i, SUBLANES), number)
+
+        def illuminate(self):
+            keep, keep8, stay8, block, lane = self.keep, self.keep8, self.stay8, self.block, self.lane
+            for i in range(0, extent, CHUNK):
+                here = slice(i, i + CHUNK)
+                shifted = []
+                for ch in range(2):
+                    turned = [
+                        pltpu.roll(
+                            padded[ch, b, pl.ds(SUBLANES - self.row_off + i, CHUNK), :],
+                            self.col_off, 1,
+                        )
+                        for b in range(2)
+                    ]
+                    shifted.append((
+                        jnp.where(keep, turned[0], turned[1]), jnp.where(keep, turned[1], turned[0])
+                    ))
+                    rolled[lane, ch, 0, here] = shifted[ch][0]
+                    rolled[lane, ch, 1, here] = shifted[ch][1]
+                rows = self.rows(i)
+                crops = []
+                for ch in range(2):
+                    left = jnp.where(
+                        keep, image[block, ch, rows, :], image[block + 2, ch, rows, :]
                     )
-                    for b in range(2)
+                    mid = image[block + 1, ch, rows, :]
+                    if i == 0:
+                        below = self.below
+                        left8 = jnp.where(
+                            keep8, image[block, ch, below, :], image[block + 2, ch, below, :]
+                        )
+                        mid8 = image[block + 1, ch, below, :]
+                        left = jnp.concatenate(
+                            [jnp.where(stay8, left[:SUBLANES], left8), left[SUBLANES:]], 0
+                        )
+                        mid = jnp.concatenate(
+                            [jnp.where(stay8, mid[:SUBLANES], mid8), mid[SUBLANES:]], 0
+                        )
+                    crops.append((left, mid))
+                real = [
+                    shifted[0][b] * crops[0][b] - shifted[1][b] * crops[1][b] for b in range(2)
                 ]
-                shifted.append(
-                    (jnp.where(keep, turned[0], turned[1]), jnp.where(keep, turned[1], turned[0]))
-                )
-                rolled[ch, 0, here] = shifted[ch][0]
-                rolled[ch, 1, here] = shifted[ch][1]
-            rows = pl.ds(pl.multiple_of(row_at + i, SUBLANES), CHUNK)
-            crops = []
-            for ch in range(2):
-                left = jnp.where(keep, image[block, ch, rows, :], image[block + 2, ch, rows, :])
-                mid = image[block + 1, ch, rows, :]
-                if i == 0:
-                    below = pl.ds(over, SUBLANES)
-                    left8 = jnp.where(
-                        keep8, image[block, ch, below, :], image[block + 2, ch, below, :]
-                    )
-                    mid8 = image[block + 1, ch, below, :]
-                    left = jnp.concatenate(
-                        [jnp.where(stay8, left[:SUBLANES], left8), left[SUBLANES:]], 0
-                    )
-                    mid = jnp.concatenate(
-                        [jnp.where(stay8, mid[:SUBLANES], mid8), mid[SUBLANES:]], 0
-                    )
-                crops.append((left, mid))
-            for b in range(2):
-                real = shifted[0][b] * crops[0][b] - shifted[1][b] * crops[1][b]
-                imag = shifted[0][b] * crops[1][b] + shifted[1][b] * crops[0][b]
-                wave[here, b * LANES:(b + 1) * LANES] = real.astype(jnp.bfloat16)
-                wave[here, extent + b * LANES:extent + (b + 1) * LANES] = imag.astype(jnp.bfloat16)
-
-        def rightwards(table):
-            result = jnp.dot(wave[...], table[...], preferred_element_type=f32)
-            half[:extent] = result[:, :extent].astype(jnp.bfloat16)
-            half[extent:] = result[:, extent:].astype(jnp.bfloat16)
-
-        def downwards(table):
-            spectrum[...] = jnp.dot(table[...], half[...], preferred_element_type=f32)
-
-        rightwards(first)
-        downwards(second)
-        for i in range(0, extent, CHUNK):
-            here = slice(i, i + CHUNK)
-            real = spectrum[here]
-            imag = spectrum[extent + i:extent + i + CHUNK]
-            misfit = real * real + imag * imag - patterns[g, here].astype(f32)
-            wave[here, :extent] = (real * misfit).astype(jnp.bfloat16)
-            wave[here, extent:] = (imag * misfit).astype(jnp.bfloat16)
-        rightwards(second)
-        downwards(first)
-
-        for i in range(0, extent, CHUNK):
-            here = slice(i, i + CHUNK)
-            rows = pl.ds(pl.multiple_of(row_at + i, SUBLANES), CHUNK)
-            for b in range(2):
+                imag = [
+                    shifted[0][b] * crops[1][b] + shifted[1][b] * crops[0][b] for b in range(2)
+                ]
+                wave[lane, 0, here, :LANES] = (real[0] + real[1]).astype(jnp.bfloat16)
+                wave[lane, 0, here, LANES:] = (imag[0] + imag[1]).astype(jnp.bfloat16)
+                wave[lane, 1, here, :LANES] = (real[0] - real[1]).astype(jnp.bfloat16)
+                wave[lane, 1, here, LANES:] = (imag[0] - imag[1]).astype(jnp.bfloat16)
+
+        def along_rows(self):
+            lane = self.lane
+            for q in range(2):
+                freq = jnp.dot(wave[lane, q], table[q], preferred_element_type=f32)
+                near, far = freq[:mid_row], freq[mid_row:]
+                cols = slice(q * LANES, (q + 1) * LANES)
+                for r, value in enumerate((near + far, near - far)):
+                    half[lane, r, :mid_row, cols] = value[:, :LANES].astype(jnp.bfloat16)
+                    half[lane, r, mid_row:, cols] = value[:, LANES:].astype(jnp.bfloat16)
+
+        def along_columns(self, at, r):
+            return jnp.dot(table[at + r], half[self.lane, r], preferred_element_type=f32)
+
+        def push(self):
+            lane = self.lane
+            for r in range(2):
+                freq = self.along_columns(6, r)
+                for i in range(0, mid_row, GROUP):
+                    here = slice(r * mid_row + i, r * mid_row + i + GROUP)
+                    real = freq[2 * i:2 * i + GROUP]
+                    imag = freq[2 * i + GROUP:2 * i + 2 * GROUP]
+                    misfit = real * real + imag * imag - patterns[self.g, here].astype(f32)
+                    real = (real * misfit).astype(jnp.bfloat16)
+                    imag = (imag * misfit).astype(jnp.bfloat16)
+                    for q in range(2):
+                        cols = slice(q * LANES, (q + 1) * LANES)
+                        wave[lane, q, here, :LANES] = real[:, cols]
+                        wave[lane, q, here, LANES:] = imag[:, cols]
+
+        def back_along_rows(self):
+            lane = self.lane
+            even = jnp.dot(wave[lane, 0], table[2], preferred_element_type=f32)
+            odd = jnp.dot(wave[lane, 1], table[3], preferred_element_type=f32)
+            for b, value in enumerate((even + odd, even - odd)):
                 cols = slice(b * LANES, (b + 1) * LANES)
-                real = spectrum[here, cols]
-                imag = spectrum[extent + i:extent + i + CHUNK, cols]
-                p_real = rolled[0, b, here]
-                p_imag = rolled[1, b, here]
-                parts = (p_real * real + p_imag * imag, p_real * imag - p_imag * real)
-                for ch in range(2):
-                    value = parts[ch]
-                    if i == 0:
-                        spill = jnp.where(stay8, 0.0, value[:SUBLANES])
-                        value = jnp.concatenate(
-                            [jnp.where(stay8, value[:SUBLANES], 0.0), value[SUBLANES:]], 0
-                        )
-                        below = pl.ds(over, SUBLANES)
+                for r in range(2):
+                    rows = slice(r * mid_row, (r + 1) * mid_row)
+                    half[lane, r, :mid_row, cols] = value[rows, :LANES].astype(jnp.bfloat16)
+                    half[lane, r, mid_row:, cols] = value[rows, LANES:].astype(jnp.bfloat16)
+
+        def gather(self):
+            keep, keep8, stay8 = self.keep[:GROUP], self.keep8, self.stay8
+            block, lane = self.block, self.lane
+            even, odd = self.along_columns(4, 0), self.along_columns(4, 1)
+            for i in range(0, extent, GROUP):
+                here = slice(i, i + GROUP)
+                rows = self.rows(i, GROUP)
+                both = jnp.add if i < mid_row else jnp.subtract
+                at = 2 * (i % mid_row)
+                for b in range(2):
+                    cols = slice(b * LANES, (b + 1) * LANES)
+                    real = both(even[at:at + GROUP, cols], odd[at:at + GROUP, cols])
+                    at_imag = slice(at + GROUP, at + 2 * GROUP)
+                    imag = both(even[at_imag, cols], odd[at_imag, cols])
+                    p_real = rolled[lane, 0, b, here]
+                    p_imag = rolled[lane, 1, b, here]
+                    parts = (p_real * real + p_imag * imag, p_real * imag - p_imag * real)
+                    for ch in range(2):
+                        value = parts[ch]
+                        if i == 0:
+                            spill = jnp.where(stay8, 0.0, value[:SUBLANES])
+                            value = jnp.concatenate(
+                                [jnp.where(stay8, value[:SUBLANES], 0.0), value[SUBLANES:]], 0
+                            )
+                            below = self.below
+                            if b == 0:
+                                grad[block, ch, below, :] += jnp.where(keep8, spill, 0.0)
+                                grad[block + 2, ch, below, :] += jnp.where(keep8, 0.0, spill)
+                            else:
+                                grad[block + 1, ch, below, :] += spill
                         if b == 0:
-                            grad[block, ch, below, :] += jnp.where(keep8, spill, 0.0)
-                            grad[block + 2, ch, below, :] += jnp.where(keep8, 0.0, spill)
+                            grad[block, ch, rows, :] += jnp.where(keep, value, 0.0)
+                            grad[block + 2, ch, rows, :] += jnp.where(keep, 0.0, value)
                         else:
-                            grad[block + 1, ch, below, :] += spill
-                    if b == 0:
-                        grad[block, ch, rows, :] += jnp.where(keep, value, 0.0)
-                        grad[block + 2, ch, rows, :] += jnp.where(keep, 0.0, value)
-                    else:
-                        grad[block + 1, ch, rows, :] += value
+                            grad[block + 1, ch, rows, :] += value
+
+        def stages(self):
+            return (
+                self.illuminate,
+                self.along_rows,
+                self.push,
+                self.back_along_rows,
+                self.gather,
+            )
+
+    def pair(p, carry):
+        ahead, behind = Slot(2 * p, 0).stages(), Slot(2 * p + 1, 1).stages()
+        for a, b in zip(ahead, behind):
+            a()
+            b()
         return carry
 
-    lax.fori_loop(0, counts[0], slot, 0)
+    live = counts[0]
+    lax.fori_loop(0, lax.div(live, 2), pair, 0)
+
+    @pl.when(lax.rem(live, 2) == 1)
+    def _():
+        for stage in Slot(live - 1, 0).stages():
+            stage()
 
     for ch in range(2):
         for i in range(BAND):
@@ -174,7 +245,7 @@
                 )
 
 
-def slot_gradients(tile, halo, probe, patterns, corners, counts, first, second):
+def slot_gradients(tile, halo, probe, patterns, corners, counts, table):
     extent = probe.shape[1]
     edge = tile.shape[1]
     total = edge + extent
@@ -185,22 +256,21 @@
     return pl.pallas_call(
         slots_kernel,
         out_shape=jax.ShapeDtypeStruct((2, BAND * BAND, extent, extent), bf16),
-        in_specs=[smem, smem] + [vmem] * 6,
+        in_specs=[smem, smem] + [vmem] * 5,
         out_specs=vmem,
         scratch_shapes=[
             pltpu.VMEM((blocks, 2, total, LANES), f32),
             pltpu.VMEM((blocks, 2, total, LANES), f32),
             pltpu.VMEM((2, 2, extent + SUBLANES, LANES), f32),
-            pltpu.VMEM((2, 2, extent, LANES), f32),
-            pltpu.VMEM((extent, 2 * extent), bf16),
-            pltpu.VMEM((2 * extent, extent), bf16),
-            pltpu.VMEM((2 * extent, extent), f32),
+            pltpu.VMEM((2, 2, 2, extent, LANES), f32),
+            pltpu.VMEM((2, 2, extent, extent), bf16),
+            pltpu.VMEM((2, 2, extent, extent), bf16),
         ],
         compiler_params=pltpu.CompilerParams(vmem_limit_bytes=40 * 1024 * 1024),
         cost_estimate=pl.CostEstimate(
             flops=4 * 4 * 2 * extent**3 * 2, bytes_accessed=8 * 2**20, transcendentals=0
         ),
-    )(corners, counts, tile, halo, probe, patterns, first, second)
+    )(corners, counts, tile, halo, probe, patterns, table)
 
 
 class Place:
@@ -231,14 +301,14 @@
 
     def leaves(self, steps):
         ends = self.local + steps
-        return jnp.logical_and(self.core == 1, jnp.logical_or(ends < 0, ends >= PLANE))
+        return jnp.logical_or(ends < 0, ends >= PLANE)
 
 
 def greet(place, extra=()):
     devices = [place.sibling(), place.chip(PLANE), place.chip(-PLANE), *extra]
-    for steps in (1, TILE_COLS, TILE_COLS + 1):
-        for sign in (1, -1):
-            devices += [place.chip(sign * steps), place.in_plane(sign * steps)]
+    for sign in (1, -1):
+        devices += [place.in_plane(sign)]
+        devices += [place.chip(sign * steps) for steps in (1, TILE_COLS, TILE_COLS + 1)]
     barrier = pltpu.get_barrier_semaphore()
     for device in devices:
         pl.semaphore_signal(barrier, inc=1, device_id=device, device_id_type=MESH)
@@ -314,6 +384,17 @@
             self.onward.wait_send()
 
 
+def along(place, steps, source, target, via, at, direct_sems, via_sems, on_sems):
+    if abs(steps) > 1:
+        return remote(source, target, direct_sems, at, place.chip(steps))
+    return Routed(place, steps, source, target, via, at, direct_sems, via_sems, on_sems)
+
+
+def hand_on(copy):
+    if isinstance(copy, Routed):
+        copy.hand_on()
+
+
 def block_of(ref, channel, i, j, extent):
     return ref.at[channel, i * extent:(i + 1) * extent, j * extent:(j + 1) * extent]
 
@@ -323,7 +404,7 @@
 
 def send_halos(place, copies, i, j, outgoing, halo, via, halo_sems, via_sems, on_sems):
     for piece, steps in halo_targets(i, j):
-        copies[piece] = Routed(
+        copies[piece] = along(
             place, steps, outgoing.at[2 * i + j], halo.at[place.core, piece], via, piece,
             halo_sems, via_sems, on_sems,
         )
@@ -343,7 +424,9 @@
         copy.wait_send()
 
 
-def first_halo_kernel(tile, halo, outgoing, via, halo_sems, via_sems, on_sems, pass_sems):
+def first_halo_kernel(
+    tile, patterns, split, halo, ordered, outgoing, via, halo_sems, via_sems, on_sems, pass_sems,
+):
     place = Place()
     extent = outgoing.shape[-1]
     greet(place)
@@ -351,8 +434,18 @@
     for i, j in ((1, 0), (0, 0), (0, 1)):
         outgoing[2 * i + j] = block_of(tile, place.core, i, j, extent)[...].astype(jnp.bfloat16)
         send_halos(place, copies, i, j, outgoing, halo, via, halo_sems, via_sems, on_sems)
+
+    def reorder(g, carry):
+        by_columns = jnp.dot(patterns[g], split[0], preferred_element_type=jnp.float32)
+        by_rows = jnp.dot(
+            split[1], by_columns.astype(jnp.bfloat16), preferred_element_type=jnp.float32
+        )
+        ordered[g] = by_rows.astype(jnp.bfloat16)
+        return carry
+
+    lax.fori_loop(0, patterns.shape[0], reorder, 0)
     for piece in HALO_ORDER:
-        copies[piece].hand_on()
+        hand_on(copies[piece])
     pass_halos(place, halo, copies, pass_sems)
 
 
@@ -394,15 +487,15 @@
     for k, (m, steps) in margins.items():
         pair_copies[k].wait_recv()
         edges[m] = (grads[core, k].astype(f32) + pair[k].astype(f32)).astype(bf16)
-        edge_copies[m] = Routed(
+        edge_copies[m] = along(
             place, steps, edges.at[m], edges_in.at[m], edges_via, m,
             edge_sems, edge_via_sems, edge_on_sems,
         )
         edge_copies[m].start()
-    edge_copies[1].hand_on()
+    hand_on(edge_copies[1])
     send_sum(1, 0)
     for m in (3, 0, 4, 2):
-        edge_copies[m].hand_on()
+        hand_on(edge_copies[m])
     send_sum(0, 0)
     send_sum(0, 1)
 
@@ -426,10 +519,10 @@
                 halo_sems, halo_via_sems, halo_on_sems,
             )
             if (i, j) == (0, 0):
-                halo_copies[RIGHT + 1].hand_on()
+                hand_on(halo_copies[RIGHT + 1])
     if not last:
         for piece in HALO_ORDER[1:]:
-            halo_copies[piece].hand_on()
+            hand_on(halo_copies[piece])
     for i, j in order:
         at = 2 * i + j
         total_copies[at].wait_recv()
@@ -447,13 +540,17 @@
     return pltpu.SemaphoreType.DMA((2, count))
 
 
-def first_halo(tile, extent):
+def first_halo(tile, patterns, split):
+    extent = patterns.shape[-1]
     vmem = pl.BlockSpec(memory_space=pltpu.VMEM)
     return pl.pallas_call(
         first_halo_kernel,
-        out_shape=jax.ShapeDtypeStruct((2, PIECES, extent, extent), jnp.bfloat16),
-        in_specs=[vmem],
-        out_specs=vmem,
+        out_shape=(
+            jax.ShapeDtypeStruct((2, PIECES, extent, extent), jnp.bfloat16),
+            jax.ShapeDtypeStruct(patterns.shape, patterns.dtype),
+        ),
+        in_specs=[vmem] * 3,
+        out_specs=(vmem,) * 2,
         scratch_shapes=[
             pltpu.VMEM((4, extent, extent), jnp.bfloat16),
             pltpu.VMEM((PIECES, extent, extent), jnp.bfloat16),
@@ -465,7 +562,7 @@
         compiler_params=pltpu.CompilerParams(
             collective_id=0, has_side_effects=True, vmem_limit_bytes=40 * 1024 * 1024
         ),
-    )(tile)
+    )(tile, patterns, split)
 
 
 def reduce_and_update(grads, tile, last):
@@ -501,10 +598,10 @@
 def shards(object_tiles, probe, patterns, corners, counts):
     tile = object_tiles[0]
     extent = probe.shape[1]
-    first, second = tables(extent)
-    halo = first_halo(tile, extent)
+    table, split = tables(extent)
+    halo, ordered = first_halo(tile, patterns, split)
     for repeat in range(ITERS):
-        grads = slot_gradients(tile, halo, probe, patterns, corners, counts, first, second)
+        grads = slot_gradients(tile, halo, probe, ordered, corners, counts, table)
         tile, *rest = reduce_and_update(grads, tile, repeat == ITERS - 1)
         if rest:
             halo = rest[0]

time: 155 us -> 148 us (0.955)
  Pallas kernels: 150 us -> 141 us
  local copies, waits for them, and re-layouts: 3.68 us -> 5.85 us
    pallas_call x2, Pallas kernels: 119 us -> 111 us  [reduce_and_update(): pl.pallas_call(functools.partial(reduce_kernel, last), out_shape=tuple(sh...]
    unnamed x12, local copies, waits for them, and re-layouts: 3.68 us -> 5.85 us
where the time goes in v4:
time: 148 us
  Pallas kernels  141 us (95%)
  local copies, waits for them, and re-layouts  5.85 us (4%)
    pallas_call x2, Pallas kernels, reduce_and_update(): pl.pallas_call(functools.partial(reduce_kernel, last), out_shape=tuple(sh...  111 us
    pallas_call x1, Pallas kernels, first_halo(): pl.pallas_call(first_halo_kernel, out_shape=(jax.ShapeDtypeStruct((2, PIE...  22 us
    pallas_call x2, Pallas kernels, slot_gradients(): pl.pallas_call(slots_kernel, out_shape=jax.ShapeDtypeStruct((2, BAND * BA...  8.23 us
    unnamed x12, local copies, waits for them, and re-layouts  5.85 us

profile of v4, /device:TPU:1, one launch (start us, length us, event | category | flops | bytes accessed | tf_op | source)
XLA Modules:
  0.0 147.6 jit_solution(4551921776601771543)
XLA Ops:
  0.7 0.8 copy.9.corners
  1.4 0.0 copy-start
  1.4 1.6 %copy-done = f32[1,2,512,512]{3,2,1,0:T(8,128)S(1)} copy-done((f32[1,2,512,512]{3,2,1,0:T(8,128)S(1)}, f32[1,2,512,512]{3,2,1,0:T(8,128)}, u32[]{:S(2)}) %copy-start) | copy-done | bytes 2097176
  3.0 0.0 copy-start.3
  3.0 1.2 copy-done.3
  4.2 0.0 copy-start.4
  4.2 0.9 copy-done.4
  5.2 0.0 copy-start.1
  5.2 0.0 copy-start.2
  5.2 22.0 %shard_map.73 = (bf16[2,5,256,256]{3,2,1,0:T(8,128)(2,1)S(1)}, bf16[8,256,256]{2,1,0:T(8,128)(2,1)S(1)}) custom-call(f32[2,512,512]{2,1,0:T(8,128)S(1)} %bitcast.2, bf16[8,256,256]{2,1,0:T(8,128)(2,1)S(1)} %copy-done.3, bf16[2,256,256]{2,1,0:T(8,128)(2,1)S(1)} %copy-done.4), custom_call_target="tpu_custom_call" | custom-call | tf_op jit(solution)/shard_map/pallas_call | solution.py:546
  27.2 0.0 copy-done.1
  27.2 0.0 copy-done.2
  27.2 4.1 %shard_map.74.grads = bf16[2,9,256,256]{3,2,1,0:T(8,128)(2,1)S(1)} custom-call(s32[8,2]{1,0:T(8,128)S(1)} %copy.9.corners, s32[1]{0:T(128)S(6)} %copy.11.counts, f32[2,512,512]{2,1,0:T(8,128)S(1)} %bitcast.3, bf16[2,5,256,256]{3,2,1,0:T(8,128)(2,1)S(1)} %get-tuple-element.9.halo, f32[2,256,256]{2,1,0:T(8,128)S(1)} %copy-done.2, ...), custom_call_target="tpu_custom_call" | custom-call | flops 1073741824 | bytes 8388608 | tf_op jit(solution)/shard_map/pallas_call | solution.py:256
  31.3 55.4 %shard_map.75 = (f32[2,512,512]{2,1,0:T(8,128)S(1)}, bf16[2,5,256,256]{3,2,1,0:T(8,128)(2,1)S(1)}) custom-call(bf16[2,9,256,256]{3,2,1,0:T(8,128)(2,1)S(1)} %shard_map.74.grads, f32[2,512,512]{2,1,0:T(8,128)S(1)} %bitcast.4), custom_call_target="tpu_custom_call" | custom-call | tf_op jit(solution)/shard_map/pallas_call | solution.py:584
  86.7 4.1 %shard_map.76.grads = bf16[2,9,256,256]{3,2,1,0:T(8,128)(2,1)S(1)} custom-call(s32[8,2]{1,0:T(8,128)S(1)} %copy.9.corners, s32[1]{0:T(128)S(6)} %copy.11.counts, f32[2,512,512]{2,1,0:T(8,128)S(1)} %get-tuple-element.11.tile, bf16[2,5,256,256]{3,2,1,0:T(8,128)(2,1)S(1)} %get-tuple-element.12.halo, f32[2,256,256]{2,1,0:T(8,128)S(1)} %copy-done.2, ...), custom_call_target="tpu_custom_call" | custom-call | flops 1073741824 | bytes 8388608 | tf_op jit(solution)/shard_map/pallas_call | solution.py:256
  90.8 55.4 %shard_map.77 = f32[2,512,512]{2,1,0:T(8,128)S(1)} custom-call(bf16[2,9,256,256]{3,2,1,0:T(8,128)(2,1)S(1)} %shard_map.76.grads, f32[2,512,512]{2,1,0:T(8,128)S(1)} %get-tuple-element.11.tile), custom_call_target="tpu_custom_call" | custom-call | tf_op jit(solution)/shard_map/pallas_call | solution.py:584
  146.3 1.3 copy.12
Async XLA Ops:
  1.4 1.6 %copy-start = (f32[1,2,512,512]{3,2,1,0:T(8,128)S(1)}, f32[1,2,512,512]{3,2,1,0:T(8,128)}, u32[]{:S(2)}) copy-start(f32[1,2,512,512]{3,2,1,0:T(8,128)} %param.7) | copy-start | bytes 6291460
  3.0 1.2 copy-start.3
  4.2 0.9 copy-start.4
  5.2 22.0 %copy-start.1 = (bf16[8,256,256]{2,1,0:T(8,128)(2,1)S(1)}, bf16[8,256,256]{2,1,0:T(8,128)(2,1)}, u32[]{:S(2)}) copy-start(bf16[8,256,256]{2,1,0:T(8,128)(2,1)} %constant.4.clone.table) | copy-start | bytes 3145732
  5.2 22.0 %copy-start.2 = (f32[2,256,256]{2,1,0:T(8,128)S(1)}, f32[2,256,256]{2,1,0:T(8,128)}, u32[]{:S(2)}) copy-start(f32[2,256,256]{2,1,0:T(8,128)} %probe.3) | copy-start | bytes 1572868

commit v5 on v4

--- a/solution.py
+++ b/solution.py
@@ -19,6 +19,7 @@
 BAND = 3
 RIGHT, LOWER, DIAG, PIECES = 0, 2, 4, 5
 PLANE = 16
+AHEAD = 2
 MESH = pl.DeviceIdType.MESH
 
 
@@ -45,10 +46,14 @@
 
 
 def slots_kernel(
-    corners, counts, tile, halo, probe, patterns, table,
-    grad_blocks,
-    image, grad, padded, rolled, wave, half,
+    reorder, corners, counts, tile, halo, probe, patterns, table, *rest,
 ):
+    if reorder:
+        split, grad_blocks, ordered, *rest = rest
+    else:
+        grad_blocks, *rest = rest
+        ordered = patterns
+    image, grad, padded, rolled, wave, half = rest
     extent = probe.shape[1]
     edge = tile.shape[1]
     own = edge // LANES
@@ -156,7 +161,7 @@
                     here = slice(r * mid_row + i, r * mid_row + i + GROUP)
                     real = freq[2 * i:2 * i + GROUP]
                     imag = freq[2 * i + GROUP:2 * i + 2 * GROUP]
-                    misfit = real * real + imag * imag - patterns[self.g, here].astype(f32)
+                    misfit = real * real + imag * imag - ordered[self.g, here].astype(f32)
                     real = (real * misfit).astype(jnp.bfloat16)
                     imag = (imag * misfit).astype(jnp.bfloat16)
                     for q in range(2):
@@ -211,7 +216,17 @@
                         else:
                             grad[block + 1, ch, rows, :] += value
 
+        def order(self):
+            by_columns = jnp.dot(patterns[self.g], split[0], preferred_element_type=f32)
+            by_rows = jnp.dot(
+                split[1], by_columns.astype(jnp.bfloat16), preferred_element_type=f32
+            )
+            ordered[self.g] = by_rows.astype(jnp.bfloat16)
+
         def stages(self):
+            return ((self.order,) if reorder else ()) + self.steps()
+
+        def steps(self):
             return (
                 self.illuminate,
                 self.along_rows,
@@ -245,7 +260,7 @@
                 )
 
 
-def slot_gradients(tile, halo, probe, patterns, corners, counts, table):
+def slot_gradients(tile, halo, probe, patterns, corners, counts, table, split=None):
     extent = probe.shape[1]
     edge = tile.shape[1]
     total = edge + extent
@@ -253,11 +268,17 @@
     f32, bf16 = jnp.float32, jnp.bfloat16
     vmem = pl.BlockSpec(memory_space=pltpu.VMEM)
     smem = pl.BlockSpec(memory_space=pltpu.SMEM)
+    reorder = split is not None
+    shapes = [jax.ShapeDtypeStruct((2, BAND * BAND, extent, extent), bf16)]
+    operands = [corners, counts, tile, halo, probe, patterns, table]
+    if reorder:
+        shapes.append(jax.ShapeDtypeStruct(patterns.shape, patterns.dtype))
+        operands.append(split)
     return pl.pallas_call(
-        slots_kernel,
-        out_shape=jax.ShapeDtypeStruct((2, BAND * BAND, extent, extent), bf16),
-        in_specs=[smem, smem] + [vmem] * 5,
-        out_specs=vmem,
+        functools.partial(slots_kernel, reorder),
+        out_shape=tuple(shapes),
+        in_specs=[smem, smem] + [vmem] * (len(operands) - 2),
+        out_specs=(vmem,) * len(shapes),
         scratch_shapes=[
             pltpu.VMEM((blocks, 2, total, LANES), f32),
             pltpu.VMEM((blocks, 2, total, LANES), f32),
@@ -270,7 +291,7 @@
         cost_estimate=pl.CostEstimate(
             flops=4 * 4 * 2 * extent**3 * 2, bytes_accessed=8 * 2**20, transcendentals=0
         ),
-    )(corners, counts, tile, halo, probe, patterns, table)
+    )(*operands)
 
 
 class Place:
@@ -282,6 +303,7 @@
         self.other = 1 - self.core
         self.flat = lax.div(pos, 2) * self.tiles + lax.axis_index("tile")
         self.local = lax.rem(self.flat, PLANE)
+        self.column = lax.rem(self.flat + TILE_COLS + TILE_COLS // 2, TILE_COLS)
 
     def at(self, flat, core):
         return lax.rem(flat, self.tiles), lax.div(flat, self.tiles) * 2 + core
@@ -299,15 +321,34 @@
         local = lax.rem(self.local + steps + PLANE, PLANE)
         return self.at(self.flat - self.local + local, self.core)
 
+    def relayed(self, steps):
+        return abs(steps) == 1 or steps == -TILE_COLS
+
+    def legs(self, steps):
+        return self.in_plane(steps), self.chip(PLANE if steps > 0 else -PLANE)
+
+    def starts(self, steps, local):
+        if steps == 1:
+            return local == PLANE - 1
+        return jnp.logical_and(local == 0, self.core == 1)
+
     def leaves(self, steps):
-        ends = self.local + steps
-        return jnp.logical_or(ends < 0, ends >= PLANE)
+        return self.starts(steps, self.local)
+
+    def hands_on(self, steps):
+        return self.starts(steps, lax.rem(self.local - steps + PLANE, PLANE))
+
+    def has_source(self, steps):
+        return self.column != (0 if steps > 0 else TILE_COLS - 1)
+
+    def has_target(self, steps):
+        return self.column != (TILE_COLS - 1 if steps > 0 else 0)
 
 
 def greet(place, extra=()):
     devices = [place.sibling(), place.chip(PLANE), place.chip(-PLANE), *extra]
     for sign in (1, -1):
-        devices += [place.in_plane(sign)]
+        devices += [place.in_plane(sign), place.in_plane(sign * TILE_COLS)]
         devices += [place.chip(sign * steps) for steps in (1, TILE_COLS, TILE_COLS + 1)]
     barrier = pltpu.get_barrier_semaphore()
     for device in devices:
@@ -339,60 +380,56 @@
 
 class Routed:
     def __init__(self, place, steps, source, target, via, at, direct_sems, via_sems, on_sems):
+        self.target = target
         self.direct = remote(source, target, direct_sems, at, place.chip(steps))
-        self.away = remote(source, via.at[at], via_sems, at, place.in_plane(steps))
-        self.onward = pltpu.make_async_remote_copy(
-            src_ref=via.at[at],
-            dst_ref=target,
-            send_sem=on_sems.at[at],
-            recv_sem=direct_sems.at[1, at],
-            device_id=place.chip(PLANE if steps > 0 else -PLANE),
-            device_id_type=MESH,
-        )
-        self.leaves = place.leaves(steps)
-        self.hands_on = place.leaves(-steps)
+        self.sends = self.receives = True
+        if abs(steps) == 1 or abs(steps) == TILE_COLS + 1:
+            self.sends, self.receives = place.has_target(steps), place.has_source(steps)
+        self.relayed = place.relayed(steps)
+        if self.relayed:
+            first, second = place.legs(steps)
+            self.away = remote(source, via.at[at], via_sems, at, first)
+            self.onward = pltpu.make_async_remote_copy(
+                src_ref=via.at[at],
+                dst_ref=target,
+                send_sem=on_sems.at[at],
+                recv_sem=direct_sems.at[1, at],
+                device_id=second,
+                device_id_type=MESH,
+            )
+            leaves = place.leaves(steps)
+            self.leaves = jnp.logical_and(self.sends, leaves)
+            self.stays = jnp.logical_and(self.sends, jnp.logical_not(leaves))
+            self.hands_on = place.hands_on(steps)
+        else:
+            self.stays = self.sends
 
     def start(self):
-        @pl.when(self.leaves)
-        def _():
-            self.away.start()
-
-        @pl.when(jnp.logical_not(self.leaves))
-        def _():
-            self.direct.start()
+        if self.relayed:
+            pl.when(self.leaves)(self.away.start)
+        pl.when(self.stays)(self.direct.start)
 
     def hand_on(self):
-        @pl.when(self.hands_on)
-        def _():
-            self.away.wait_recv()
-            self.onward.start()
+        if self.relayed:
+
+            @pl.when(self.hands_on)
+            def _():
+                self.away.wait_recv()
+                self.onward.start()
 
     def wait_recv(self):
-        self.direct.wait_recv()
+        pl.when(self.receives)(self.direct.wait_recv)
+        if self.receives is not True:
+
+            @pl.when(jnp.logical_not(self.receives))
+            def _():
+                self.target[...] = jnp.zeros(self.target.shape, self.target.dtype)
 
     def wait_send(self):
-        @pl.when(self.leaves)
-        def _():
-            self.away.wait_send()
-
-        @pl.when(jnp.logical_not(self.leaves))
-        def _():
-            self.direct.wait_send()
-
-        @pl.when(self.hands_on)
-        def _():
-            self.onward.wait_send()
-
-
-def along(place, steps, source, target, via, at, direct_sems, via_sems, on_sems):
-    if abs(steps) > 1:
-        return remote(source, target, direct_sems, at, place.chip(steps))
-    return Routed(place, steps, source, target, via, at, direct_sems, via_sems, on_sems)
-
-
-def hand_on(copy):
-    if isinstance(copy, Routed):
-        copy.hand_on()
+        if self.relayed:
+            pl.when(self.leaves)(self.away.wait_send)
+            pl.when(self.hands_on)(self.onward.wait_send)
+        pl.when(self.stays)(self.direct.wait_send)
 
 
 def block_of(ref, channel, i, j, extent):
@@ -404,7 +441,7 @@
 
 def send_halos(place, copies, i, j, outgoing, halo, via, halo_sems, via_sems, on_sems):
     for piece, steps in halo_targets(i, j):
-        copies[piece] = along(
+        copies[piece] = Routed(
             place, steps, outgoing.at[2 * i + j], halo.at[place.core, piece], via, piece,
             halo_sems, via_sems, on_sems,
         )
@@ -425,27 +462,17 @@
 
 
 def first_halo_kernel(
-    tile, patterns, split, halo, ordered, outgoing, via, halo_sems, via_sems, on_sems, pass_sems,
+    tile, halo, outgoing, via, halo_sems, via_sems, on_sems, pass_sems,
 ):
     place = Place()
     extent = outgoing.shape[-1]
     greet(place)
     copies = {}
-    for i, j in ((1, 0), (0, 0), (0, 1)):
+    for i, j in ((0, 0), (1, 0), (0, 1)):
         outgoing[2 * i + j] = block_of(tile, place.core, i, j, extent)[...].astype(jnp.bfloat16)
         send_halos(place, copies, i, j, outgoing, halo, via, halo_sems, via_sems, on_sems)
-
-    def reorder(g, carry):
-        by_columns = jnp.dot(patterns[g], split[0], preferred_element_type=jnp.float32)
-        by_rows = jnp.dot(
-            split[1], by_columns.astype(jnp.bfloat16), preferred_element_type=jnp.float32
-        )
-        ordered[g] = by_rows.astype(jnp.bfloat16)
-        return carry
-
-    lax.fori_loop(0, patterns.shape[0], reorder, 0)
-    for piece in HALO_ORDER:
-        hand_on(copies[piece])
+    for piece in (RIGHT, RIGHT + 1, LOWER, LOWER + 1):
+        copies[piece].hand_on()
     pass_halos(place, halo, copies, pass_sems)
 
 
@@ -454,7 +481,8 @@
         halo, outgoing, halo_via, halo_sems, halo_via_sems, halo_on_sems, pass_sems = rest[:7]
         rest = rest[7:]
     (pair, edges, edges_in, edges_via, sums, sums_in, totals, totals_in,
-     pair_sems, edge_sems, edge_via_sems, edge_on_sems, sum_sems, total_sems) = rest
+     pair_sems, edge_sems, edge_via_sems, edge_on_sems,
+     sum_sems, total_sems) = rest
     place = Place()
     extent = grads.shape[-1]
     core, other = place.core, place.other
@@ -470,6 +498,7 @@
         pair_copies[k].start()
     edge_copies = {}
     sum_copies = {}
+    under_way = []
 
     def send_sum(i, j):
         k = BAND * i + j
@@ -481,23 +510,25 @@
             value = value + edges_in[m].astype(f32)
         sums[at] = value.astype(bf16)
         sum_copies[at] = remote(sums.at[at], sums_in.at[at], sum_sems, at, place.chip(across))
+        if len(under_way) >= AHEAD:
+            under_way.pop(0).wait_send()
         sum_copies[at].start()
+        under_way.append(sum_copies[at])
 
     send_sum(1, 1)
     for k, (m, steps) in margins.items():
         pair_copies[k].wait_recv()
         edges[m] = (grads[core, k].astype(f32) + pair[k].astype(f32)).astype(bf16)
-        edge_copies[m] = along(
+        edge_copies[m] = Routed(
             place, steps, edges.at[m], edges_in.at[m], edges_via, m,
             edge_sems, edge_via_sems, edge_on_sems,
         )
         edge_copies[m].start()
-    hand_on(edge_copies[1])
+    edge_copies[1].hand_on()
     send_sum(1, 0)
-    for m in (3, 0, 4, 2):
-        hand_on(edge_copies[m])
-    send_sum(0, 0)
-    send_sum(0, 1)
+    edge_copies[0].hand_on()
+    for i, j in order[2:]:
+        send_sum(i, j)
 
     total_copies = {}
     halo_copies = {}
@@ -519,10 +550,10 @@
                 halo_sems, halo_via_sems, halo_on_sems,
             )
             if (i, j) == (0, 0):
-                hand_on(halo_copies[RIGHT + 1])
+                for piece in (RIGHT + 1, LOWER, RIGHT):
+                    halo_copies[piece].hand_on()
     if not last:
-        for piece in HALO_ORDER[1:]:
-            hand_on(halo_copies[piece])
+        halo_copies[LOWER + 1].hand_on()
     for i, j in order:
         at = 2 * i + j
         total_copies[at].wait_recv()
@@ -531,26 +562,21 @@
         ] - LEARNING_RATE * totals_in[at].astype(f32)
     if not last:
         pass_halos(place, halo, halo_copies, pass_sems)
-    for group in (pair_copies, edge_copies, sum_copies, total_copies):
-        for copy in group.values():
-            copy.wait_send()
+    for copy in (*pair_copies.values(), *edge_copies.values(), *under_way, *total_copies.values()):
+        copy.wait_send()
 
 
 def sems(count):
     return pltpu.SemaphoreType.DMA((2, count))
 
 
-def first_halo(tile, patterns, split):
-    extent = patterns.shape[-1]
+def first_halo(tile, extent):
     vmem = pl.BlockSpec(memory_space=pltpu.VMEM)
     return pl.pallas_call(
         first_halo_kernel,
-        out_shape=(
-            jax.ShapeDtypeStruct((2, PIECES, extent, extent), jnp.bfloat16),
-            jax.ShapeDtypeStruct(patterns.shape, patterns.dtype),
-        ),
-        in_specs=[vmem] * 3,
-        out_specs=(vmem,) * 2,
+        out_shape=jax.ShapeDtypeStruct((2, PIECES, extent, extent), jnp.bfloat16),
+        in_specs=[vmem],
+        out_specs=vmem,
         scratch_shapes=[
             pltpu.VMEM((4, extent, extent), jnp.bfloat16),
             pltpu.VMEM((PIECES, extent, extent), jnp.bfloat16),
@@ -562,7 +588,7 @@
         compiler_params=pltpu.CompilerParams(
             collective_id=0, has_side_effects=True, vmem_limit_bytes=40 * 1024 * 1024
         ),
-    )(tile, patterns, split)
+    )(tile)
 
 
 def reduce_and_update(grads, tile, last):
@@ -579,8 +605,9 @@
         shapes.append(jax.ShapeDtypeStruct((2, PIECES, extent, extent), jnp.bfloat16))
         scratch += [blocks(4), blocks(PIECES), sems(PIECES), sems(PIECES), onward, sems(PIECES)]
     scratch += [blocks(BAND * BAND), blocks(PIECES), blocks(PIECES), blocks(PIECES)]
-    scratch += [blocks(4), blocks(4), blocks(4), blocks(4)]
-    scratch += [sems(BAND * BAND), sems(PIECES), sems(PIECES), onward, sems(4), sems(4)]
+    scratch += [blocks(4)] * 4
+    scratch += [sems(BAND * BAND), sems(PIECES), sems(PIECES), onward]
+    scratch += [sems(4), sems(4)]
     return pl.pallas_call(
         functools.partial(reduce_kernel, last),
         out_shape=tuple(shapes),
@@ -599,9 +626,13 @@
     tile = object_tiles[0]
     extent = probe.shape[1]
     table, split = tables(extent)
-    halo, ordered = first_halo(tile, patterns, split)
+    halo = first_halo(tile, extent)
     for repeat in range(ITERS):
-        grads = slot_gradients(tile, halo, probe, ordered, corners, counts, table)
+        grads, *ordered = slot_gradients(
+            tile, halo, probe, patterns, corners, counts, table, None if repeat else split
+        )
+        if ordered:
+            patterns = ordered[0]
         tile, *rest = reduce_and_update(grads, tile, repeat == ITERS - 1)
         if rest:
             halo = rest[0]

time: 148 us -> 144 us (0.973)
  the two profiles are of different devices: /device:TPU:1 before, /device:TPU:73 now
where the time goes in v5:
time: 144 us
  Pallas kernels  139 us (97%)
  local copies, waits for them, and re-layouts  3.68 us (3%)
    pallas_call x2, Pallas kernels, reduce_and_update(): pl.pallas_call(functools.partial(reduce_kernel, last), out_shape=tuple(sh...  114 us
    pallas_call x1, Pallas kernels, first_halo(): pl.pallas_call(first_halo_kernel, out_shape=jax.ShapeDtypeStruct((2, PIEC...  17.1 us
    pallas_call x2, Pallas kernels, slot_gradients(): pl.pallas_call(functools.partial(slots_kernel, reorder), out_shape=tuple(...  8.41 us
    unnamed x12, local copies, waits for them, and re-layouts  3.68 us

profile of v5, /device:TPU:73, one launch (start us, length us, event | category | flops | bytes accessed | tf_op | source)
XLA Modules:
  0.0 143.7 jit_solution(17252215513541786923)
XLA Ops:
  0.7 0.8 copy.9.corners
  1.4 0.0 copy-start
  1.4 1.6 %copy-done = f32[1,2,512,512]{3,2,1,0:T(8,128)S(1)} copy-done((f32[1,2,512,512]{3,2,1,0:T(8,128)S(1)}, f32[1,2,512,512]{3,2,1,0:T(8,128)}, u32[]{:S(2)}) %copy-start) | copy-done | bytes 2097176
  3.0 0.0 copy-start.1
  3.0 0.0 copy-start.2
  3.0 0.0 copy-start.3
  3.0 0.0 copy-start.4
  3.0 17.1 %shard_map.73.halo = bf16[2,5,256,256]{3,2,1,0:T(8,128)(2,1)S(1)} custom-call(f32[2,512,512]{2,1,0:T(8,128)S(1)} %bitcast.2), custom_call_target="tpu_custom_call" | custom-call | tf_op jit(solution)/shard_map/pallas_call | solution.py:575
  20.1 0.0 copy-done.1
  20.1 0.0 copy-done.2
  20.1 0.0 copy-done.3
  20.1 0.0 copy-done.4
  20.1 4.3 %shard_map.74 = (bf16[2,9,256,256]{3,2,1,0:T(8,128)(2,1)S(1)}, bf16[8,256,256]{2,1,0:T(8,128)(2,1)S(1)}) custom-call(s32[8,2]{1,0:T(8,128)S(1)} %copy.9.corners, s32[1]{0:T(128)S(6)} %copy.11.counts, f32[2,512,512]{2,1,0:T(8,128)S(1)} %bitcast.3, bf16[2,5,256,256]{3,2,1,0:T(8,128)(2,1)S(1)} %shard_map.73.halo, f32[2,256,256]{2,1,0:T(8,128)S(1)} %copy-done.2, ...), custom_call_target="tpu_custom_call" | custom-call | flops 1073741824 | bytes 8388608 | tf_op jit(solution)/shard_map/pallas_call | solution.py:277
  24.5 50.9 %shard_map.75 = (f32[2,512,512]{2,1,0:T(8,128)S(1)}, bf16[2,5,256,256]{3,2,1,0:T(8,128)(2,1)S(1)}) custom-call(bf16[2,9,256,256]{3,2,1,0:T(8,128)(2,1)S(1)} %get-tuple-element.9.grads, f32[2,512,512]{2,1,0:T(8,128)S(1)} %bitcast.4), custom_call_target="tpu_custom_call" | custom-call | tf_op jit(solution)/shard_map/pallas_call | solution.py:611
  75.4 4.1 %shard_map.76.grads = bf16[2,9,256,256]{3,2,1,0:T(8,128)(2,1)S(1)} custom-call(s32[8,2]{1,0:T(8,128)S(1)} %copy.9.corners, s32[1]{0:T(128)S(6)} %copy.11.counts, f32[2,512,512]{2,1,0:T(8,128)S(1)} %get-tuple-element.10.tile, bf16[2,5,256,256]{3,2,1,0:T(8,128)(2,1)S(1)} %get-tuple-element.11.halo, f32[2,256,256]{2,1,0:T(8,128)S(1)} %copy-done.2, ...), custom_call_target="tpu_custom_call" | custom-call | flops 1073741824 | bytes 8388608 | tf_op jit(solution)/shard_map/pallas_call | solution.py:277
  79.5 62.9 %shard_map.77 = f32[2,512,512]{2,1,0:T(8,128)S(1)} custom-call(bf16[2,9,256,256]{3,2,1,0:T(8,128)(2,1)S(1)} %shard_map.76.grads, f32[2,512,512]{2,1,0:T(8,128)S(1)} %get-tuple-element.10.tile), custom_call_target="tpu_custom_call" | custom-call | tf_op jit(solution)/shard_map/pallas_call | solution.py:611
  142.4 1.3 copy.12
Async XLA Ops:
  1.4 1.6 %copy-start = (f32[1,2,512,512]{3,2,1,0:T(8,128)S(1)}, f32[1,2,512,512]{3,2,1,0:T(8,128)}, u32[]{:S(2)}) copy-start(f32[1,2,512,512]{3,2,1,0:T(8,128)} %param.7) | copy-start | bytes 6291460
  3.0 17.1 %copy-start.1 = (bf16[8,256,256]{2,1,0:T(8,128)(2,1)S(1)}, bf16[8,256,256]{2,1,0:T(8,128)(2,1)}, u32[]{:S(2)}) copy-start(bf16[8,256,256]{2,1,0:T(8,128)(2,1)} %constant.4.clone.table) | copy-start | bytes 3145732
  3.0 17.1 %copy-start.2 = (f32[2,256,256]{2,1,0:T(8,128)S(1)}, f32[2,256,256]{2,1,0:T(8,128)}, u32[]{:S(2)}) copy-start(f32[2,256,256]{2,1,0:T(8,128)} %probe.3) | copy-start | bytes 1572868
  3.0 17.1 %copy-start.3 = (bf16[8,256,256]{2,1,0:T(8,128)(2,1)S(1)}, bf16[8,256,256]{2,1,0:T(8,128)(2,1)}, u32[]{:S(2)}) copy-start(bf16[8,256,256]{2,1,0:T(8,128)(2,1)} %patterns.1) | copy-start | bytes 3145732
  3.0 17.1 %copy-start.4 = (bf16[2,256,256]{2,1,0:T(8,128)(2,1)S(1)}, bf16[2,256,256]{2,1,0:T(8,128)(2,1)}, u32[]{:S(2)}) copy-start(bf16[2,256,256]{2,1,0:T(8,128)(2,1)} %constant.5.clone.rest_0_) | copy-start | bytes 786436

commit v6 on v5

--- a/solution.py
+++ b/solution.py
@@ -322,15 +322,13 @@
         return self.at(self.flat - self.local + local, self.core)
 
     def relayed(self, steps):
-        return abs(steps) == 1 or steps == -TILE_COLS
+        return abs(steps) == 1
 
     def legs(self, steps):
         return self.in_plane(steps), self.chip(PLANE if steps > 0 else -PLANE)
 
     def starts(self, steps, local):
-        if steps == 1:
-            return local == PLANE - 1
-        return jnp.logical_and(local == 0, self.core == 1)
+        return jnp.logical_and(local == (PLANE - 1 if steps > 0 else 0), self.core == 1)
 
     def leaves(self, steps):
         return self.starts(steps, self.local)
@@ -348,7 +346,7 @@
 def greet(place, extra=()):
     devices = [place.sibling(), place.chip(PLANE), place.chip(-PLANE), *extra]
     for sign in (1, -1):
-        devices += [place.in_plane(sign), place.in_plane(sign * TILE_COLS)]
+        devices += [place.in_plane(sign)]
         devices += [place.chip(sign * steps) for steps in (1, TILE_COLS, TILE_COLS + 1)]
     barrier = pltpu.get_barrier_semaphore()
     for device in devices:

time: 144 us -> 139 us (0.965)
  the two profiles are of different devices: /device:TPU:73 before, /device:TPU:27 now
where the time goes in v6:
time: 139 us
  Pallas kernels  135 us (97%)
  local copies, waits for them, and re-layouts  3.68 us (3%)
    pallas_call x2, Pallas kernels, reduce_and_update(): pl.pallas_call(functools.partial(reduce_kernel, last), out_shape=tuple(sh...  105 us
    pallas_call x1, Pallas kernels, first_halo(): pl.pallas_call(first_halo_kernel, out_shape=jax.ShapeDtypeStruct((2, PIEC...  23.5 us
    pallas_call x2, Pallas kernels, slot_gradients(): pl.pallas_call(functools.partial(slots_kernel, reorder), out_shape=tuple(...  6.25 us
    unnamed x12, local copies, waits for them, and re-layouts  3.68 us

profile of v6, /device:TPU:27, one launch (start us, length us, event | category | flops | bytes accessed | tf_op | source)
XLA Modules:
  0.0 139.2 jit_solution(12141737708335528036)
XLA Ops:
  0.7 0.8 copy.9.corners
  1.4 0.0 copy-start
  1.4 1.6 %copy-done = f32[1,2,512,512]{3,2,1,0:T(8,128)S(1)} copy-done((f32[1,2,512,512]{3,2,1,0:T(8,128)S(1)}, f32[1,2,512,512]{3,2,1,0:T(8,128)}, u32[]{:S(2)}) %copy-start) | copy-done | bytes 2097176
  3.0 0.0 copy-start.1
  3.0 0.0 copy-start.2
  3.0 0.0 copy-start.3
  3.0 0.0 copy-start.4
  3.0 23.5 %shard_map.73.halo = bf16[2,5,256,256]{3,2,1,0:T(8,128)(2,1)S(1)} custom-call(f32[2,512,512]{2,1,0:T(8,128)S(1)} %bitcast.2), custom_call_target="tpu_custom_call" | custom-call | tf_op jit(solution)/shard_map/pallas_call | solution.py:573
  26.5 0.0 copy-done.1
  26.5 0.0 copy-done.2
  26.5 0.0 copy-done.3
  26.6 0.0 copy-done.4
  26.6 3.2 %shard_map.74 = (bf16[2,9,256,256]{3,2,1,0:T(8,128)(2,1)S(1)}, bf16[8,256,256]{2,1,0:T(8,128)(2,1)S(1)}) custom-call(s32[8,2]{1,0:T(8,128)S(1)} %copy.9.corners, s32[1]{0:T(128)S(6)} %copy.11.counts, f32[2,512,512]{2,1,0:T(8,128)S(1)} %bitcast.3, bf16[2,5,256,256]{3,2,1,0:T(8,128)(2,1)S(1)} %shard_map.73.halo, f32[2,256,256]{2,1,0:T(8,128)S(1)} %copy-done.2, ...), custom_call_target="tpu_custom_call" | custom-call | flops 1073741824 | bytes 8388608 | tf_op jit(solution)/shard_map/pallas_call | solution.py:277
  29.7 55.0 %shard_map.75 = (f32[2,512,512]{2,1,0:T(8,128)S(1)}, bf16[2,5,256,256]{3,2,1,0:T(8,128)(2,1)S(1)}) custom-call(bf16[2,9,256,256]{3,2,1,0:T(8,128)(2,1)S(1)} %get-tuple-element.9.grads, f32[2,512,512]{2,1,0:T(8,128)S(1)} %bitcast.4), custom_call_target="tpu_custom_call" | custom-call | tf_op jit(solution)/shard_map/pallas_call | solution.py:609
  84.7 3.1 %shard_map.76.grads = bf16[2,9,256,256]{3,2,1,0:T(8,128)(2,1)S(1)} custom-call(s32[8,2]{1,0:T(8,128)S(1)} %copy.9.corners, s32[1]{0:T(128)S(6)} %copy.11.counts, f32[2,512,512]{2,1,0:T(8,128)S(1)} %get-tuple-element.10.tile, bf16[2,5,256,256]{3,2,1,0:T(8,128)(2,1)S(1)} %get-tuple-element.11.halo, f32[2,256,256]{2,1,0:T(8,128)S(1)} %copy-done.2, ...), custom_call_target="tpu_custom_call" | custom-call | flops 1073741824 | bytes 8388608 | tf_op jit(solution)/shard_map/pallas_call | solution.py:277
  87.8 50.1 %shard_map.77 = f32[2,512,512]{2,1,0:T(8,128)S(1)} custom-call(bf16[2,9,256,256]{3,2,1,0:T(8,128)(2,1)S(1)} %shard_map.76.grads, f32[2,512,512]{2,1,0:T(8,128)S(1)} %get-tuple-element.10.tile), custom_call_target="tpu_custom_call" | custom-call | tf_op jit(solution)/shard_map/pallas_call | solution.py:609
  137.9 1.3 copy.12
Async XLA Ops:
  1.4 1.6 %copy-start = (f32[1,2,512,512]{3,2,1,0:T(8,128)S(1)}, f32[1,2,512,512]{3,2,1,0:T(8,128)}, u32[]{:S(2)}) copy-start(f32[1,2,512,512]{3,2,1,0:T(8,128)} %param.7) | copy-start | bytes 6291460
  3.0 23.5 %copy-start.1 = (bf16[8,256,256]{2,1,0:T(8,128)(2,1)S(1)}, bf16[8,256,256]{2,1,0:T(8,128)(2,1)}, u32[]{:S(2)}) copy-start(bf16[8,256,256]{2,1,0:T(8,128)(2,1)} %constant.4.clone.table) | copy-start | bytes 3145732
  3.0 23.5 %copy-start.2 = (f32[2,256,256]{2,1,0:T(8,128)S(1)}, f32[2,256,256]{2,1,0:T(8,128)}, u32[]{:S(2)}) copy-start(f32[2,256,256]{2,1,0:T(8,128)} %probe.3) | copy-start | bytes 1572868
  3.0 23.5 %copy-start.3 = (bf16[8,256,256]{2,1,0:T(8,128)(2,1)S(1)}, bf16[8,256,256]{2,1,0:T(8,128)(2,1)}, u32[]{:S(2)}) copy-start(bf16[8,256,256]{2,1,0:T(8,128)(2,1)} %patterns.1) | copy-start | bytes 3145732
  3.0 23.6 %copy-start.4 = (bf16[2,256,256]{2,1,0:T(8,128)(2,1)S(1)}, bf16[2,256,256]{2,1,0:T(8,128)(2,1)}, u32[]{:S(2)}) copy-start(bf16[2,256,256]{2,1,0:T(8,128)(2,1)} %constant.5.clone.rest_0_) | copy-start | bytes 786436
